TPU v7x, 32 devices: a whole 2x2x4 slice. The times are simulated.
32 devices in a mesh: ctx: 16 (over z, y, x), tp: 2 (over core).
Axes of the slice: x: 2, y: 2, z: 4, core: 2. Of those that a mesh axis runs over, the one named last changes fastest.
Arguments:
- gate_out: bfloat16 [8192, 4096], P('ctx', 'tp'), may hold values from -6 to 6
- gate_in: bfloat16 [8192, 4096], P('ctx', 'tp'), may hold values from -6 to 6
- signal: bfloat16 [8192, 4096], P('ctx', 'tp'), may hold values from -6 to 6
- decay_rates: float32 [16, 4096], P(None, 'tp'), may hold values from 3.90625e-06 to 0.1, as said below
- residues: float32 [16, 4096], P(None, 'tp'), may hold values from -0.6 to 0.6
- skip_gain: float32 [4096], P('tp'), may hold values from -4 to 4
- out_proj: bfloat16 [4096, 4096], P('tp'), may hold values from -0.09375 to 0.09375
- doc_lengths: int32 [8], replicated, may hold values from 1 to 5120, 8192 in all
Outputs:
- layer_out: bfloat16 [8192, 4096], P(('ctx', 'tp'))
Inputs may be any that keep to these rules, and one draw needn't show every extreme that they name: `doc_lengths`: 8 documents laid end to end, lengths summing to 8192. `decay_rates`: positive.
All inputs are finite; a program needn't handle non-finite values.
Results may differ from a plain program's by a relative error of at most 0.017.
Values may be sent and summed in bfloat16 or wider, within the bound.
A program may use at most 128 MiB of HBM per device.

v0:
```python
import jax
import jax.numpy as jnp
from jax import lax
from jax.sharding import PartitionSpec as P

precise = lax.Precision.HIGHEST


def per_device(gate_out, gate_in, signal, decay_rates, residues, skip_gain, out_proj, doc_lengths):
    length = signal.shape[0]
    channels = signal.shape[1]
    block_len = min(32, length)
    num_blocks = length // block_len
    my_shard = lax.axis_index("ctx")
    shard_begin = my_shard * length
    doc_ends = jnp.cumsum(doc_lengths)
    doc_starts = doc_ends - doc_lengths
    positions = shard_begin + jnp.arange(length, dtype=jnp.int32)
    doc_index = jnp.sum((doc_starts[None, :] <= positions[:, None]).astype(jnp.int32), axis=1)
    opening = jnp.any(doc_starts[None, :] == positions[:, None], axis=1)
    head_start = jnp.max(jnp.where(doc_starts <= shard_begin, doc_starts, 0))
    open_shard = ((doc_index == doc_index[0]) & (head_start < shard_begin)).astype(jnp.float32)
    anchor = head_start // length
    feed_in = gate_in.astype(jnp.float32) * signal.astype(jnp.float32)
    lag_steps = jnp.arange(block_len, dtype=jnp.float32)
    lag_decay = jnp.exp(-lag_steps[None, :, None] * decay_rates[:, None, :])
    filter_taps = jnp.einsum("nkc,nc->kc", lag_decay, residues, precision=precise)
    lag_ids = jnp.arange(block_len, dtype=jnp.int32)
    onehot = (lag_ids[:, None, None] - lag_ids[None, :, None] == lag_ids[None, None, :]).astype(
        jnp.float32
    )
    toeplitz = jnp.einsum("tsk,kc->tsc", onehot, filter_taps, precision=precise)
    enter_decay = jnp.exp(-(lag_steps + 1.0)[None, :, None] * decay_rates[:, None, :])
    leave_decay = jnp.exp(-(block_len - 1.0 - lag_steps)[None, :, None] * decay_rates[:, None, :])
    block_decay = jnp.exp(-block_len * decay_rates)

    def advance(carry_state, inputs):
        block_rows, block_docs, block_marks = inputs
        same_doc = (block_docs[:, None] == block_docs[None, :]).astype(jnp.float32)
        within = jnp.einsum(
            "tsc,sc->tc", toeplitz * same_doc[:, :, None], block_rows, precision=precise
        )
        before = (jnp.cumsum(block_marks.astype(jnp.int32)) == 0).astype(jnp.float32)
        incoming = (
            jnp.einsum("ntc,nc->tc", enter_decay, residues * carry_state, precision=precise)
            * before[:, None]
        )
        tail_mask = (block_docs == block_docs[block_len - 1]).astype(jnp.float32)
        passes = 1.0 - jnp.max(block_marks.astype(jnp.float32))
        added_state = jnp.einsum(
            "nsc,s,sc->nc", leave_decay, tail_mask, block_rows, precision=precise
        )
        return (block_decay * carry_state * passes + added_state, within + incoming)

    zero_state = jnp.zeros((decay_rates.shape[0], channels), jnp.float32)
    end_state, local_out = lax.scan(
        advance,
        zero_state,
        (
            feed_in.reshape(num_blocks, block_len, channels),
            doc_index.reshape(num_blocks, block_len),
            opening.reshape(num_blocks, block_len),
        ),
    )
    local_out = local_out.reshape(length, channels)
    states_part = lax.all_gather(end_state[None], "ctx", axis=0, tiled=True)
    row_count = states_part.shape[0]
    shard_ids = jnp.arange(row_count, dtype=jnp.int32)
    shard_gap = jnp.maximum(my_shard - 1 - shard_ids, 0).astype(jnp.float32)
    in_window = ((shard_ids >= anchor) & (shard_ids < my_shard)).astype(jnp.float32)
    weight = (
        jnp.exp(-(length * shard_gap)[:, None, None] * decay_rates[None, :, :])
        * in_window[:, None, None]
    )
    carried = jnp.sum(weight * states_part, axis=0)
    offsets = jnp.arange(1, length + 1, dtype=jnp.float32)
    decay_out = jnp.exp(-offsets[None, :, None] * decay_rates[:, None, :])
    from_prior = (
        jnp.einsum("ntc,nc->tc", decay_out, residues * carried, precision=precise)
        * open_shard[:, None]
    )
    conv_total = local_out + from_prior + skip_gain[None, :] * feed_in
    hidden = (gate_out.astype(jnp.float32) * conv_total).astype(jnp.bfloat16)
    return lax.psum_scatter(
        jnp.dot(hidden, out_proj, preferred_element_type=jnp.float32).astype(jnp.bfloat16),
        "tp",
        scatter_dimension=0,
        tiled=True,
    )


def solution(mesh):
    return jax.shard_map(
        per_device,
        mesh=mesh,
        in_specs=(
            P("ctx", "tp"),
            P("ctx", "tp"),
            P("ctx", "tp"),
            P(None, "tp"),
            P(None, "tp"),
            P("tp"),
            P("tp", None),
            P(),
        ),
        out_specs=P(("ctx", "tp"), None),
        check_vma=False,
    )
```

profile of v0, /device:TPU:31, one launch (start us, length us, event | category | flops | bytes accessed | tf_op | source)
XLA Modules:
  0.0 338.1 jit_solution(9516121359513073405)
XLA Ops:
  7.4 1.3 fusion.11
  10.0 1.7 multiply_reduce_fusion.4
  11.7 5.7 %fusion.8 = f32[32,32,2048]{2,1,0:T(8,128)} fusion(f32[2048,32]{0,1:T(8,128)S(1)} %multiply_reduce_fusion.4, s32[32,32]{1,0:T(8,128)S(1)} %iota_subtract_fusion), kind=kOutput, calls=%fused_computation.28 | convolution fusion | flops 805339136 | bytes 8654848 | tf_op jit(solution)/shard_map/tsk,kc->tsc/dot_general | solution.py:32
  17.4 2.8 convert_multiply_fusion
  20.2 202.1 %while.15 = (s32[]{:T(128)}, f32[16,2048]{1,0:T(8,128)S(1)}, f32[16,32,2048]{2,1,0:T(8,128)}, f32[16,2048]{1,0:T(8,128)S(1)}, pred[16,32]{1,0:T(8,128)(4,1)S(1)}...) while((s32[]{:T(128)}, f32[16,2048]{1,0:T(8,128)S(1)}, ...), condition=%wide.region_6.7_spmd.clone.clone.clone, body=%wide.region_3.6_spmd.clone.clone.clone.sunk | while | flops 12782787 | bytes 12594199 | solution.py:56
  21.6 1.0 fusion.17
  25.9 1.0 dynamic-slice_bitcast_fusion.2
  26.9 4.9 %multiply_reduce_fusion.10 = f32[2048,32]{0,1:T(8,128)S(1)} fusion(f32[32,32,2048]{2,1,0:T(8,128)} %get-tuple-element.318, f32[2048,32]{0,1:T(8,128)S(1)} %dynamic-slice_bitcast_fusion.2, f32[32,32]{1,0:T(8,128)S(1)} %compare_convert_fusion.5), kind=kLoop, calls=%fused_computation.2.clone.1 | loop fusion | flops 6225920 | bytes 8916992 | tf_op jit(solution)/shard_map/while/body/eval_jaxpr/tsc,sc->tc/dot_general | solution.py:40
  34.2 1.0 fusion.17
  35.3 1.0 multiply_reduce_fusion.9
  38.5 1.0 dynamic-slice_bitcast_fusion.2
  39.5 4.9 %multiply_reduce_fusion.10 = f32[2048,32]{0,1:T(8,128)S(1)} fusion(f32[32,32,2048]{2,1,0:T(8,128)} %get-tuple-element.318, f32[2048,32]{0,1:T(8,128)S(1)} %dynamic-slice_bitcast_fusion.2, f32[32,32]{1,0:T(8,128)S(1)} %compare_convert_fusion.5), kind=kLoop, calls=%fused_computation.2.clone.1 | loop fusion | flops 6225920 | bytes 8916992 | tf_op jit(solution)/shard_map/while/body/eval_jaxpr/tsc,sc->tc/dot_general | solution.py:40
  46.9 1.0 fusion.17
  51.2 1.0 dynamic-slice_bitcast_fusion.2
  52.1 4.9 %multiply_reduce_fusion.10 = f32[2048,32]{0,1:T(8,128)S(1)} fusion(f32[32,32,2048]{2,1,0:T(8,128)} %get-tuple-element.318, f32[2048,32]{0,1:T(8,128)S(1)} %dynamic-slice_bitcast_fusion.2, f32[32,32]{1,0:T(8,128)S(1)} %compare_convert_fusion.5), kind=kLoop, calls=%fused_computation.2.clone.1 | loop fusion | flops 6225920 | bytes 8916992 | tf_op jit(solution)/shard_map/while/body/eval_jaxpr/tsc,sc->tc/dot_general | solution.py:40
  59.5 1.0 fusion.17
  63.8 1.0 dynamic-slice_bitcast_fusion.2
  64.8 4.9 %multiply_reduce_fusion.10 = f32[2048,32]{0,1:T(8,128)S(1)} fusion(f32[32,32,2048]{2,1,0:T(8,128)} %get-tuple-element.318, f32[2048,32]{0,1:T(8,128)S(1)} %dynamic-slice_bitcast_fusion.2, f32[32,32]{1,0:T(8,128)S(1)} %compare_convert_fusion.5), kind=kLoop, calls=%fused_computation.2.clone.1 | loop fusion | flops 6225920 | bytes 8916992 | tf_op jit(solution)/shard_map/while/body/eval_jaxpr/tsc,sc->tc/dot_general | solution.py:40
  72.1 1.0 fusion.17
  76.4 1.0 dynamic-slice_bitcast_fusion.2
  77.4 4.9 %multiply_reduce_fusion.10 = f32[2048,32]{0,1:T(8,128)S(1)} fusion(f32[32,32,2048]{2,1,0:T(8,128)} %get-tuple-element.318, f32[2048,32]{0,1:T(8,128)S(1)} %dynamic-slice_bitcast_fusion.2, f32[32,32]{1,0:T(8,128)S(1)} %compare_convert_fusion.5), kind=kLoop, calls=%fused_computation.2.clone.1 | loop fusion | flops 6225920 | bytes 8916992 | tf_op jit(solution)/shard_map/while/body/eval_jaxpr/tsc,sc->tc/dot_general | solution.py:40
  84.7 1.0 fusion.17
  89.0 1.0 dynamic-slice_bitcast_fusion.2
  90.0 4.9 %multiply_reduce_fusion.10 = f32[2048,32]{0,1:T(8,128)S(1)} fusion(f32[32,32,2048]{2,1,0:T(8,128)} %get-tuple-element.318, f32[2048,32]{0,1:T(8,128)S(1)} %dynamic-slice_bitcast_fusion.2, f32[32,32]{1,0:T(8,128)S(1)} %compare_convert_fusion.5), kind=kLoop, calls=%fused_computation.2.clone.1 | loop fusion | flops 6225920 | bytes 8916992 | tf_op jit(solution)/shard_map/while/body/eval_jaxpr/tsc,sc->tc/dot_general | solution.py:40
  97.4 1.0 fusion.17
  98.4 1.0 multiply_reduce_fusion.9
  101.7 1.0 dynamic-slice_bitcast_fusion.2
  102.6 4.9 %multiply_reduce_fusion.10 = f32[2048,32]{0,1:T(8,128)S(1)} fusion(f32[32,32,2048]{2,1,0:T(8,128)} %get-tuple-element.318, f32[2048,32]{0,1:T(8,128)S(1)} %dynamic-slice_bitcast_fusion.2, f32[32,32]{1,0:T(8,128)S(1)} %compare_convert_fusion.5), kind=kLoop, calls=%fused_computation.2.clone.1 | loop fusion | flops 6225920 | bytes 8916992 | tf_op jit(solution)/shard_map/while/body/eval_jaxpr/tsc,sc->tc/dot_general | solution.py:40
  110.0 1.0 fusion.17
  111.0 1.0 multiply_reduce_fusion.9
  114.3 1.0 dynamic-slice_bitcast_fusion.2
  115.3 4.9 %multiply_reduce_fusion.10 = f32[2048,32]{0,1:T(8,128)S(1)} fusion(f32[32,32,2048]{2,1,0:T(8,128)} %get-tuple-element.318, f32[2048,32]{0,1:T(8,128)S(1)} %dynamic-slice_bitcast_fusion.2, f32[32,32]{1,0:T(8,128)S(1)} %compare_convert_fusion.5), kind=kLoop, calls=%fused_computation.2.clone.1 | loop fusion | flops 6225920 | bytes 8916992 | tf_op jit(solution)/shard_map/while/body/eval_jaxpr/tsc,sc->tc/dot_general | solution.py:40
  122.6 1.0 fusion.17
  123.6 1.0 multiply_reduce_fusion.9
  126.9 1.0 dynamic-slice_bitcast_fusion.2
  127.9 4.9 %multiply_reduce_fusion.10 = f32[2048,32]{0,1:T(8,128)S(1)} fusion(f32[32,32,2048]{2,1,0:T(8,128)} %get-tuple-element.318, f32[2048,32]{0,1:T(8,128)S(1)} %dynamic-slice_bitcast_fusion.2, f32[32,32]{1,0:T(8,128)S(1)} %compare_convert_fusion.5), kind=kLoop, calls=%fused_computation.2.clone.1 | loop fusion | flops 6225920 | bytes 8916992 | tf_op jit(solution)/shard_map/while/body/eval_jaxpr/tsc,sc->tc/dot_general | solution.py:40
  135.2 1.0 fusion.17
  136.3 1.0 multiply_reduce_fusion.9
  139.5 1.0 dynamic-slice_bitcast_fusion.2
  140.5 4.9 %multiply_reduce_fusion.10 = f32[2048,32]{0,1:T(8,128)S(1)} fusion(f32[32,32,2048]{2,1,0:T(8,128)} %get-tuple-element.318, f32[2048,32]{0,1:T(8,128)S(1)} %dynamic-slice_bitcast_fusion.2, f32[32,32]{1,0:T(8,128)S(1)} %compare_convert_fusion.5), kind=kLoop, calls=%fused_computation.2.clone.1 | loop fusion | flops 6225920 | bytes 8916992 | tf_op jit(solution)/shard_map/while/body/eval_jaxpr/tsc,sc->tc/dot_general | solution.py:40
  147.9 1.0 fusion.17
  152.2 1.0 dynamic-slice_bitcast_fusion.2
  153.1 4.9 %multiply_reduce_fusion.10 = f32[2048,32]{0,1:T(8,128)S(1)} fusion(f32[32,32,2048]{2,1,0:T(8,128)} %get-tuple-element.318, f32[2048,32]{0,1:T(8,128)S(1)} %dynamic-slice_bitcast_fusion.2, f32[32,32]{1,0:T(8,128)S(1)} %compare_convert_fusion.5), kind=kLoop, calls=%fused_computation.2.clone.1 | loop fusion | flops 6225920 | bytes 8916992 | tf_op jit(solution)/shard_map/while/body/eval_jaxpr/tsc,sc->tc/dot_general | solution.py:40
  160.5 1.0 fusion.17
  164.8 1.0 dynamic-slice_bitcast_fusion.2
  165.8 4.9 %multiply_reduce_fusion.10 = f32[2048,32]{0,1:T(8,128)S(1)} fusion(f32[32,32,2048]{2,1,0:T(8,128)} %get-tuple-element.318, f32[2048,32]{0,1:T(8,128)S(1)} %dynamic-slice_bitcast_fusion.2, f32[32,32]{1,0:T(8,128)S(1)} %compare_convert_fusion.5), kind=kLoop, calls=%fused_computation.2.clone.1 | loop fusion | flops 6225920 | bytes 8916992 | tf_op jit(solution)/shard_map/while/body/eval_jaxpr/tsc,sc->tc/dot_general | solution.py:40
  173.1 1.0 fusion.17
  177.4 1.0 dynamic-slice_bitcast_fusion.2
  178.4 4.9 %multiply_reduce_fusion.10 = f32[2048,32]{0,1:T(8,128)S(1)} fusion(f32[32,32,2048]{2,1,0:T(8,128)} %get-tuple-element.318, f32[2048,32]{0,1:T(8,128)S(1)} %dynamic-slice_bitcast_fusion.2, f32[32,32]{1,0:T(8,128)S(1)} %compare_convert_fusion.5), kind=kLoop, calls=%fused_computation.2.clone.1 | loop fusion | flops 6225920 | bytes 8916992 | tf_op jit(solution)/shard_map/while/body/eval_jaxpr/tsc,sc->tc/dot_general | solution.py:40
  185.8 1.0 fusion.17
  190.1 1.0 dynamic-slice_bitcast_fusion.2
  191.0 4.9 %multiply_reduce_fusion.10 = f32[2048,32]{0,1:T(8,128)S(1)} fusion(f32[32,32,2048]{2,1,0:T(8,128)} %get-tuple-element.318, f32[2048,32]{0,1:T(8,128)S(1)} %dynamic-slice_bitcast_fusion.2, f32[32,32]{1,0:T(8,128)S(1)} %compare_convert_fusion.5), kind=kLoop, calls=%fused_computation.2.clone.1 | loop fusion | flops 6225920 | bytes 8916992 | tf_op jit(solution)/shard_map/while/body/eval_jaxpr/tsc,sc->tc/dot_general | solution.py:40
  198.4 1.0 fusion.17
  202.7 1.0 dynamic-slice_bitcast_fusion.2
  203.7 4.9 %multiply_reduce_fusion.10 = f32[2048,32]{0,1:T(8,128)S(1)} fusion(f32[32,32,2048]{2,1,0:T(8,128)} %get-tuple-element.318, f32[2048,32]{0,1:T(8,128)S(1)} %dynamic-slice_bitcast_fusion.2, f32[32,32]{1,0:T(8,128)S(1)} %compare_convert_fusion.5), kind=kLoop, calls=%fused_computation.2.clone.1 | loop fusion | flops 6225920 | bytes 8916992 | tf_op jit(solution)/shard_map/while/body/eval_jaxpr/tsc,sc->tc/dot_general | solution.py:40
  211.0 1.0 fusion.17
  215.3 1.0 dynamic-slice_bitcast_fusion.2
  216.3 4.9 %multiply_reduce_fusion.10 = f32[2048,32]{0,1:T(8,128)S(1)} fusion(f32[32,32,2048]{2,1,0:T(8,128)} %get-tuple-element.318, f32[2048,32]{0,1:T(8,128)S(1)} %dynamic-slice_bitcast_fusion.2, f32[32,32]{1,0:T(8,128)S(1)} %compare_convert_fusion.5), kind=kLoop, calls=%fused_computation.2.clone.1 | loop fusion | flops 6225920 | bytes 8916992 | tf_op jit(solution)/shard_map/while/body/eval_jaxpr/tsc,sc->tc/dot_general | solution.py:40
  227.2 54.7 %all-gather.3.cloned.1.call-done = f32[256,2048]{1,0:T(8,128)} async-done(((f32[16,2048]{1,0:T(8,128)}), f32[256,2048]{1,0:T(8,128)}) %all-gather.3.cloned.1.call-update) | async-done | bytes 2097168 | tf_op jit(solution)/shard_map/all_gather | solution.py:66
  281.9 2.1 multiply_reduce_fusion.5
  284.1 14.5 %multiply_reduce_fusion.3 = f32[2048,512]{0,1:T(8,128)} fusion(f32[2048,16]{0,1:T(8,128)S(1)} %multiply_bitcast_fusion.1, f32[16,2048]{1,0:T(8,128)S(1)} %get-tuple-element.334, f32[512]{0:T(512)S(1)} %add_negate_fusion), kind=kLoop, calls=%fused_computation.18 | loop fusion | flops 49283072 | bytes 4458496 | tf_op jit(solution)/shard_map/ntc,nc->tc/dot_general | solution.py:79
  298.6 4.4 %fusion.7 = bf16[512,2048]{1,0:T(8,128)(2,1)S(1)} fusion(f32[16,32,2048]{2,1,0:T(8,128)S(1)} %copy-done.5, f32[2048,512]{0,1:T(8,128)} %multiply_reduce_fusion.3, bf16[512,2048]{1,0:T(8,128)(2,1)S(1)} %copy-done.6, f32[2048]{0:T(1024)S(1)} %copy-done.8, f32[512]{0:T(512)S(1)} %and_convert_fusion, bf16[512,2048]{1,0:T(8,128)(2,1)S(1)} %copy-done, ...), kind=kLoop, calls=%fused_computation.23 | loop fusion | flops 10485760 | bytes 16787456 | tf_op jit(solution)/shard_map/convert_element_type | solution.py:83
  303.0 13.8 %convolution_convert_fusion = bf16[512,4096]{1,0:T(8,128)(2,1)} fusion(bf16[512,2048]{1,0:T(8,128)(2,1)S(1)} %fusion.7, bf16[2048,4096]{1,0:T(8,128)(2,1)} %param.16), kind=kOutput, calls=%fused_computation.19 | convolution fusion | flops 8592031744 | bytes 23068672 | tf_op jit(solution)/shard_map/dot_general | solution.py:85
  316.9 14.4 %reduce-scatter.2.cloned.1.call-done = bf16[256,4096]{1,0:T(8,128)(2,1)} async-done(((bf16[512,4096]{1,0:T(8,128)(2,1)}), bf16[256,4096]{1,0:T(8,128)(2,1)}) %reduce-scatter.2.cloned.1.call-update) | async-done | bytes 2097168 | tf_op jit(solution)/shard_map/reduce_scatter | solution.py:84
  (259 shorter events, 79.3 us)
Async XLA Ops:
  6.5 275.4 %all-gather.3.cloned.1.call-start = ((), (), s32[]{:S(2)}) async-start(), calls=%async_computation.2 | async-start | bytes 2228224 | tf_op jit(solution)/shard_map/all_gather | solution.py:66
  11.7 5.7 %copy-start = (bf16[512,2048]{1,0:T(8,128)(2,1)S(1)}, bf16[512,2048]{1,0:T(8,128)(2,1)}, u32[]{:S(2)}) copy-start(bf16[512,2048]{1,0:T(8,128)(2,1)} %param.12) | copy-start | bytes 6291460
  11.7 5.7 %copy-start.1 = (bf16[512,2048]{1,0:T(8,128)(2,1)S(1)}, bf16[512,2048]{1,0:T(8,128)(2,1)}, u32[]{:S(2)}) copy-start(bf16[512,2048]{1,0:T(8,128)(2,1)} %param.11) | copy-start | bytes 6291460
  17.4 2.8 copy-start.3
  17.4 2.8 copy-start.7
  222.3 0.7 copy-start.4
  223.0 108.3 %reduce-scatter.2.cloned.1.call-start = ((), (), s32[]{:S(2)}) async-start(), calls=%async_computation.1 | async-start | bytes 6291456 | tf_op jit(solution)/shard_map/reduce_scatter | solution.py:84
  284.0 14.5 %copy-start.2 = (bf16[512,2048]{1,0:T(8,128)(2,1)S(1)}, bf16[512,2048]{1,0:T(8,128)(2,1)}, u32[]{:S(2)}) copy-start(bf16[512,2048]{1,0:T(8,128)(2,1)} %param.11) | copy-start | bytes 6291460
  284.0 14.5 %copy-start.5 = (f32[16,32,2048]{2,1,0:T(8,128)S(1)}, f32[16,32,2048]{2,1,0:T(8,128)}, u32[]{:S(2)}) copy-start(f32[16,32,2048]{2,1,0:T(8,128)} %get-tuple-element.63) | copy-start | bytes 12582916
  284.0 14.5 %copy-start.6 = (bf16[512,2048]{1,0:T(8,128)(2,1)S(1)}, bf16[512,2048]{1,0:T(8,128)(2,1)}, u32[]{:S(2)}) copy-start(bf16[512,2048]{1,0:T(8,128)(2,1)} %param.10) | copy-start | bytes 6291460
  284.1 14.5 %copy-start.8 = (f32[2048]{0:T(1024)S(1)}, f32[2048]{0:T(1024)}, u32[]{:S(2)}) copy-start(f32[2048]{0:T(1024)} %param.15) | copy-start | bytes 24580
Sparse Core Ops, SparseCore 0:
  223.1 58.7 all-gather.2
  317.0 14.2 reduce-scatter.1
where the time goes:
time: 341 us; the launch traced here: 338 us
  other arithmetic  192 us (56%)
  waiting for transfers between devices  69.1 us (20%)
  local copies, waits for them, and re-layouts  29.2 us (9%)
  matrix products  19.5 us (6%)
  between operations  16.4 us (5%)
  loops' own time  11.9 us (3%)
    dot_general x16, other arithmetic, advance(): jnp.einsum('tsc,sc->tc', toeplitz * same_doc[:, :, None], block_rows, pre...  78.1 us
    all_gather x1, waiting for transfers between devices, per_device(): states_part = lax.all_gather(end_state[None], 'ctx', axis=0, tiled=True)  54.7 us
    while x32, other arithmetic  18 us
    while x16, local copies, waits for them, and re-layouts  15.5 us
    dot_general x16, other arithmetic, advance(): jnp.einsum('nsc,s,sc->nc', leave_decay, tail_mask, block_rows, precision=...  15.2 us
    dot_general x1, other arithmetic, per_device(): jnp.einsum('ntc,nc->tc', decay_out, residues * carried, precision=precise)  14.5 us
    reduce_scatter x1, waiting for transfers between devices, per_device(): lax.psum_scatter(jnp.dot(hidden, out_proj, preferred_element_type=jnp.flo...  14.4 us
    dot_general x1, matrix products, per_device(): jnp.dot(hidden, out_proj, preferred_element_type=jnp.float32)  13.8 us
  transfers between devices with their start and end apart: 2, of which 2 were waited for; matrix products, arithmetic and copies ran while one was open for 0% of the time, Pallas kernels for 0%

commit v1 on v0

v1 whole, which is shorter than its diff:
```python
import functools

import jax
import jax.numpy as jnp
from jax import lax
from jax.experimental import pallas as pl
from jax.experimental.pallas import tpu as pltpu
from jax.sharding import PartitionSpec as P

LANES = 128
SUB = 8
STEP = 8
CHUNK = 64


def spread(x_ref, gate_ref, sig_ref, q, q8, keep=None):
    rows = gate_ref.shape[0]

    def tile(i, _):
        t0 = pl.multiple_of(i * 16, 16)
        for j in range(q):
            cols = pl.ds(j * LANES, LANES)
            x = gate_ref[pl.ds(t0, 16), cols].astype(jnp.float32) * sig_ref[
                pl.ds(t0, 16), cols
            ].astype(jnp.float32)
            if keep is not None:
                x = x * keep(t0)
            x_ref[pl.ds(t0 * q8 + j, 16, stride=q8), :] = x
        return 0

    lax.fori_loop(0, rows // 16, tile, 0)


def end_state_kernel(modes, q, q8, last_ref, gate_ref, sig_ref, decay_ref, end_ref, x_ref, s_ref):
    step = pl.program_id(0)
    rows = gate_ref.shape[0]

    @pl.when(step == 0)
    def _():
        s_ref[...] = jnp.zeros_like(s_ref)

    last = last_ref[0]
    base = step * rows

    def keep(t0):
        at = base + t0 + lax.broadcasted_iota(jnp.int32, (16, LANES), 0)
        return (at >= last).astype(jnp.float32)

    @pl.when(base + rows > last)
    def _():
        spread(x_ref, gate_ref, sig_ref, q, q8, keep)
        for h in range(0, q8, SUB):
            d = [decay_ref[n, pl.ds(h, SUB), :] for n in range(modes)]

            def block(i, s):
                s = list(s)
                for k in range(STEP):
                    at = pl.multiple_of((i * STEP + k) * q8 + h, SUB)
                    x = x_ref[pl.ds(at, SUB), :]
                    for n in range(modes):
                        s[n] = d[n] * s[n] + x
                return tuple(s)

            out = lax.fori_loop(
                0, rows // STEP, block, tuple(s_ref[n, pl.ds(h, SUB), :] for n in range(modes))
            )
            for n in range(modes):
                s_ref[n, pl.ds(h, SUB), :] = out[n]

    @pl.when(step == pl.num_programs(0) - 1)
    def _():
        end_ref[...] = s_ref[...].astype(end_ref.dtype)


def exchange_kernel(n, length, plan, end_ref, rate_ref, mask_ref, out_ref, send_buf, slots, send_sem, recv_sem):
    me = lax.axis_index("ctx")
    offsets = sorted({off for stage in plan for off, _ in stage})
    barrier = pltpu.get_barrier_semaphore()
    for off in offsets:

        @pl.when(me >= off)
        def _():
            pl.semaphore_signal(
                barrier, inc=1, device_id={"ctx": me - off}, device_id_type=pl.DeviceIdType.MESH
            )

    peers = sum((me + off < n).astype(jnp.int32) for off in offsets)

    @pl.when(me + 1 < n)
    def _():
        pl.semaphore_wait(barrier, peers)

    def copy(k, stage, off):
        src = end_ref if stage == 0 else send_buf.at[stage - 1]
        return pltpu.make_async_remote_copy(
            src_ref=src,
            dst_ref=slots.at[k],
            send_sem=send_sem.at[k],
            recv_sem=recv_sem.at[k],
            device_id={"ctx": jnp.minimum(me + off, n - 1)},
            device_id_type=pl.DeviceIdType.MESH,
        )

    out_ref[...] = jnp.zeros_like(out_ref)
    k0 = 0
    for stage, hops in enumerate(plan):
        if stage:
            send_buf[stage - 1] = out_ref[...].astype(send_buf.dtype)
        for k, (off, gap) in enumerate(hops, k0):

            @pl.when(me + off < n)
            def _():
                copy(k, stage, off).start()

        for k, (off, gap) in enumerate(hops, k0):

            @pl.when(me >= off)
            def _():
                weight = jnp.exp(rate_ref[...] * (-float(length * gap))) * mask_ref[pl.ds(k, 1), :]
                copy(k, stage, off).wait_recv()
                out_ref[...] += weight * slots[k].astype(jnp.float32)

        k0 += len(hops)
    k = 0
    for stage, hops in enumerate(plan):
        for off, gap in hops:

            @pl.when(me + off < n)
            def _():
                copy(k, stage, off).wait_send()

            k += 1


def conv_kernel(
    modes, q, q8, keep_ref, cut_ref, go_ref, gate_ref, sig_ref, decay_ref, res_ref, skip_ref,
    carried_ref, hidden_ref, x_ref, y_ref, s_ref,
):
    step = pl.program_id(0)
    rows = gate_ref.shape[0]

    @pl.when(step == 0)
    def _():
        s_ref[...] = carried_ref[...]

    spread(x_ref, gate_ref, sig_ref, q, q8)
    for h in range(0, q8, SUB):
        d = [decay_ref[n, pl.ds(h, SUB), :] for n in range(modes)]
        r = [res_ref[n, pl.ds(h, SUB), :] for n in range(modes)]
        skip = skip_ref[pl.ds(h, SUB), :]

        def run(i, s, cut):
            s = list(s)
            for k in range(STEP):
                at = pl.multiple_of((i * STEP + k) * q8 + h, SUB)
                x = x_ref[pl.ds(at, SUB), :]
                parts = [skip * x, None, None, None]
                if cut:
                    keep = keep_ref[step * rows + i * STEP + k]
                for n in range(modes):
                    old = s[n] * keep if cut else s[n]
                    s[n] = d[n] * old + x
                    term = r[n] * s[n]
                    p = parts[n % 4]
                    parts[n % 4] = term if p is None else p + term
                y_ref[pl.ds(at, SUB), :] = (parts[0] + parts[1]) + (parts[2] + parts[3])
            return tuple(s)

        def block(i, s):
            return lax.cond(
                cut_ref[step * (rows // STEP) + i] > 0,
                lambda s: run(i, s, True),
                lambda s: run(i, s, False),
                s,
            )

        out = lax.fori_loop(
            0, rows // STEP, block, tuple(s_ref[n, pl.ds(h, SUB), :] for n in range(modes))
        )
        for n in range(modes):
            s_ref[n, pl.ds(h, SUB), :] = out[n]

    def tile(i, _):
        t0 = pl.multiple_of(i * 16, 16)
        for j in range(q):
            cols = pl.ds(j * LANES, LANES)
            y = y_ref[pl.ds(t0 * q8 + j, 16, stride=q8), :]
            g = go_ref[pl.ds(t0, 16), cols].astype(jnp.float32)
            hidden_ref[pl.ds(t0, 16), cols] = (g * y).astype(hidden_ref.dtype)
        return 0

    lax.fori_loop(0, rows // 16, tile, 0)


def scan_plan(n):
    plan = [[(off, off - 1) for off in range(1, min(4, n - 1) + 1)]]
    unit = 4
    while unit < n:
        plan.append([(off, off) for off in (unit, 2 * unit, 3 * unit) if off < n])
        unit *= 4
    return plan


def make(n, tp):
    plan = scan_plan(n)
    hops = sum(len(stage) for stage in plan)

    def per_device(gate_out, gate_in, signal, decay_rates, residues, skip_gain, out_proj, doc_lengths):
        length, channels = signal.shape
        modes = decay_rates.shape[0]
        q = channels // LANES
        q8 = -(-q // SUB) * SUB
        chunk = min(CHUNK, length)
        me = lax.axis_index("ctx")
        begin = me * length
        doc_starts = jnp.cumsum(doc_lengths) - doc_lengths
        local = doc_starts - begin
        inside = (local >= 0) & (local < length)
        last = jnp.max(jnp.where(inside, local, 0)).astype(jnp.int32).reshape(1)
        at = jnp.arange(length, dtype=jnp.int32)
        opening = jnp.any(local[None, :] == at[:, None], axis=1)
        keep = 1.0 - opening.astype(jnp.float32)
        cut = jnp.max(opening.reshape(length // STEP, STEP).astype(jnp.int32), axis=1)
        head = jnp.max(jnp.where(doc_starts <= begin, doc_starts, 0))
        ids = jnp.array([gap for stage in plan for _, gap in stage], jnp.int32)
        mask = (head < (me - ids) * length).astype(jnp.float32)
        mask = jnp.broadcast_to(mask[:, None], (hops, LANES))

        def fold(a):
            a = a.reshape(a.shape[:-1] + (q, LANES))
            if q8 > q:
                a = jnp.pad(a, [(0, 0)] * (a.ndim - 2) + [(0, q8 - q), (0, 0)])
            return a

        rates = fold(decay_rates)
        decay = jnp.exp(-rates)
        res = fold(residues)
        skip = fold(skip_gain)
        smem = pl.BlockSpec(memory_space=pltpu.SMEM)
        rows = pl.BlockSpec((chunk, channels), lambda i: (i, 0))
        whole = pl.BlockSpec((modes, q8, LANES), lambda i: (0, 0, 0))
        end = pl.pallas_call(
            functools.partial(end_state_kernel, modes, q, q8),
            grid=(length // chunk,),
            out_shape=jax.ShapeDtypeStruct((modes, q8, LANES), jnp.bfloat16),
            in_specs=[smem, rows, rows, whole],
            out_specs=whole,
            scratch_shapes=[
                pltpu.VMEM((chunk * q8, LANES), jnp.float32),
                pltpu.VMEM((modes, q8, LANES), jnp.float32),
            ],
            compiler_params=pltpu.CompilerParams(vmem_limit_bytes=16 << 20),
            name="end_state",
        )(last, gate_in, signal, decay)

        flat = (modes * q8, LANES)
        vmem = pl.BlockSpec(memory_space=pltpu.VMEM)
        carried = pl.pallas_call(
            functools.partial(exchange_kernel, n, length, plan),
            out_shape=jax.ShapeDtypeStruct(flat, jnp.float32),
            in_specs=[vmem] * 3,
            out_specs=vmem,
            scratch_shapes=[
                pltpu.VMEM((max(len(plan) - 1, 1),) + flat, jnp.bfloat16),
                pltpu.VMEM((hops,) + flat, jnp.bfloat16),
                pltpu.SemaphoreType.DMA((hops,)),
                pltpu.SemaphoreType.DMA((hops,)),
            ],
            compiler_params=pltpu.CompilerParams(
                collective_id=0, has_side_effects=True, vmem_limit_bytes=16 << 20
            ),
            name="state_exchange",
        )(end.reshape(flat), rates.reshape(flat), mask)

        hidden = pl.pallas_call(
            functools.partial(conv_kernel, modes, q, q8),
            grid=(length // chunk,),
            out_shape=jax.ShapeDtypeStruct((length, channels), jnp.bfloat16),
            in_specs=[smem, smem, rows, rows, rows, whole, whole,
                      pl.BlockSpec((q8, LANES), lambda i: (0, 0)), whole],
            out_specs=rows,
            scratch_shapes=[
                pltpu.VMEM((chunk * q8, LANES), jnp.float32),
                pltpu.VMEM((chunk * q8, LANES), jnp.float32),
                pltpu.VMEM((modes, q8, LANES), jnp.float32),
            ],
            compiler_params=pltpu.CompilerParams(vmem_limit_bytes=24 << 20),
            name="conv",
        )(keep, cut, gate_out, gate_in, signal, decay, res, skip,
          carried.reshape(modes, q8, LANES))

        def project(h):
            return jnp.dot(h, out_proj, preferred_element_type=jnp.float32).astype(jnp.bfloat16)

        if tp != 2:
            return lax.psum_scatter(project(hidden), "tp", scatter_dimension=0, tiled=True)
        half = length // 2
        core = lax.axis_index("tp")
        other = project(lax.dynamic_slice_in_dim(hidden, (1 - core) * half, half, 0))
        other = lax.ppermute(other, "tp", [(0, 1), (1, 0)])
        own = project(lax.dynamic_slice_in_dim(hidden, core * half, half, 0))
        return (own.astype(jnp.float32) + other.astype(jnp.float32)).astype(jnp.bfloat16)

    return per_device


def solution(mesh):
    return jax.shard_map(
        make(mesh.shape["ctx"], mesh.shape["tp"]),
        mesh=mesh,
        in_specs=(
            P("ctx", "tp"),
            P("ctx", "tp"),
            P("ctx", "tp"),
            P(None, "tp"),
            P(None, "tp"),
            P("tp"),
            P("tp", None),
            P(),
        ),
        out_specs=P(("ctx", "tp"), None),
        check_vma=False,
    )
```

time: 341 us -> 76.5 us (0.22)
  other arithmetic: 192 us -> 4.69 us
  waiting for transfers between devices: 69.1 us -> 4.13 us
  Pallas kernels: 0 us -> 34.4 us
  local copies, waits for them, and re-layouts: 29.2 us -> 6.82 us
  between operations: 16.4 us -> 0.1 us
  loops' own time: 11.9 us -> 0 us
  matrix products: 19.5 us -> 23.3 us
    dot_general x50 -> x0, other arithmetic: 122 us -> none  [the longest x16 78.1 us: advance(): jnp.einsum('tsc,sc->tc', toeplitz * same_doc[:, :, None], block_rows, pre...]
    all_gather x1 -> x0, waiting for transfers between devices: 54.7 us -> none  [per_device(): states_part = lax.all_gather(end_state[None], 'ctx', axis=0, tiled=True)]
    pallas_call x0 -> x3, Pallas kernels: none -> 34.4 us  [the longest x1 16.8 us: per_device(): pl.pallas_call(functools.partial(exchange_kernel, n, length, plan), out_s...]
    while x32 -> x0, other arithmetic: 18 us -> none
    while x16 -> x0, local copies, waits for them, and re-layouts: 15.5 us -> none
    reduce_scatter x1 -> x0, waiting for transfers between devices: 14.4 us -> none  [per_device(): lax.psum_scatter(jnp.dot(hidden, out_proj, preferred_element_type=jnp.flo...]
    dynamic_update_slice x16 -> x0, other arithmetic: 12.9 us -> none  [per_device(): lax.scan(advance, zero_state, (feed_in.reshape(num_blocks, block_len, cha...]
    another operation x33 -> x1, other arithmetic: 12.8 us -> 0.83 us
  transfers between devices with their start and end apart: 2 -> 1, of which waited for: 2 -> 1; matrix products, arithmetic and copies ran while one was open for 0% -> 0% of each run, Pallas kernels for 0% -> 0%
where the time goes in v1:
time: 76.5 us; the launch traced here: 76.7 us
  Pallas kernels  34.4 us (45%)
  matrix products  23.3 us (30%)
  local copies, waits for them, and re-layouts  6.82 us (9%)
  other arithmetic  4.69 us (6%)
  waiting for transfers between devices  4.13 us (5%)
  starting transfers between devices  3.29 us (4%)
    dot_general x2, matrix products, project(): jnp.dot(h, out_proj, preferred_element_type=jnp.float32)  23.3 us
    pallas_call x1, Pallas kernels, per_device(): pl.pallas_call(functools.partial(exchange_kernel, n, length, plan), out_s...  16.8 us
    pallas_call x1, Pallas kernels, per_device(): pl.pallas_call(functools.partial(conv_kernel, modes, q, q8), grid=(length...  15.1 us
    unnamed x14, local copies, waits for them, and re-layouts  5.74 us
    ppermute x1, waiting for transfers between devices, per_device(): other = lax.ppermute(other, 'tp', [(0, 1), (1, 0)])  4.13 us
    ppermute x1, starting transfers between devices, per_device(): other = lax.ppermute(other, 'tp', [(0, 1), (1, 0)])  3.29 us
    pallas_call x1, Pallas kernels, per_device(): pl.pallas_call(functools.partial(end_state_kernel, modes, q, q8), grid=(l...  2.56 us
  transfers between devices with their start and end apart: 1, of which 1 were waited for; matrix products, arithmetic and copies ran while one was open for 0% of the time, Pallas kernels for 0%

profile of v1, /device:TPU:31, one launch (start us, length us, event | category | flops | bytes accessed | tf_op | source)
XLA Modules:
  0.0 76.7 jit_solution(13858075393198419014)
XLA Ops:
  0.0 0.8 %reduce-window.9 = s32[8,1]{0,1:T(1,128)S(1)} reduce-window(s32[8,1]{0,1:T(1,128)} %bitcast.26, s32[]{:T(128)} %constant.11.clone.1), window={size=8x1 pad=7_0x0_0}, to_apply=%region_0.0 | reduce-window | flops 56 | bytes 68 | tf_op jit(solution)/shard_map/reduce-window.4
  0.8 1.4 %fusion.6 = (s32[]{:T(128)}, s32[8]{0:T(128)S(1)}, s32[]{:T(128)}) fusion(s32[]{:T(128)S(6)} %mul.12, s32[8]{0:T(128)} %param.16, s32[8,1]{0,1:T(1,128)S(1)} %reduce-window.9), kind=kLoop, calls=%fused_computation.13 | loop fusion | flops 78 | bytes 108 | tf_op jit(solution)/shard_map/reduce_max | solution.py:219
  2.2 0.1 fusion.5
  2.3 0.9 %reshape_reshape.3.rate_ref = f32[256,128]{1,0:T(8,128)S(1)} reshape(f32[16,2048]{1,0:T(8,128)} %param.12) | data formatting | bytes 262144 | tf_op jit(solution)/shard_map/reshape;reshape | solution.py:273
  3.2 0.9 %exponential_bitcast_fusion = f32[2,8,16,128]{3,1,2,0:T(8,128)S(1)} fusion(f32[16,2048]{1,0:T(8,128)} %param.12), kind=kLoop, calls=%fused_computation.6 | loop fusion | flops 32768 | bytes 262144
  4.2 0.1 reshape.56
  4.3 0.9 %copy.11 = f32[2,8,16,128]{3,2,1,0:T(8,128)S(1)} copy(f32[2,8,16,128]{3,1,2,0:T(8,128)} %bitcast.25) | data formatting | bytes 262144
  5.2 1.3 %compare_convert_fusion = f32[7]{0:T(128)S(1)} fusion(s32[7]{0:T(128)} %constant.31, s32[]{:T(128)S(6)} %axis_index.23, s32[]{:T(128)} %get-tuple-element.7), kind=kLoop, calls=%fused_computation.11 | loop fusion | flops 28 | bytes 64 | tf_op jit(solution)/shard_map/convert_element_type | solution.py:226
  6.6 0.1 reduce_max.27.cut_ref
  6.7 0.0 copy-start
  6.7 1.6 %copy-done = bf16[512,2048]{1,0:T(8,128)(2,1)S(1)} copy-done((bf16[512,2048]{1,0:T(8,128)(2,1)S(1)}, bf16[512,2048]{1,0:T(8,128)(2,1)}, u32[]{:S(2)}) %copy-start) | copy-done | bytes 2097176
  8.3 0.0 copy-start.2
  8.3 1.6 %copy-done.2 = bf16[512,2048]{1,0:T(8,128)(2,1)S(1)} copy-done((bf16[512,2048]{1,0:T(8,128)(2,1)S(1)}, bf16[512,2048]{1,0:T(8,128)(2,1)}, u32[]{:S(2)}) %copy-start.2) | copy-done | bytes 2097176
  9.9 0.0 copy-start.1
  9.9 0.0 copy-start.3
  9.9 0.0 copy-start.5
  9.9 2.6 %end_state.1 = bf16[16,16,128]{2,1,0:T(8,128)(2,1)S(1)} custom-call(s32[1]{0:T(128)} %bitcast.3.last_ref, bf16[512,2048]{1,0:T(8,128)(2,1)S(1)} %copy-done, bf16[512,2048]{1,0:T(8,128)(2,1)S(1)} %copy-done.2, f32[16,16,128]{2,1,0:T(8,128)S(1)} %bitcast.19), custom_call_target="tpu_custom_call" | custom-call | tf_op jit(solution)/shard_map/end_state/pallas_call | solution.py:242
  12.5 0.1 broadcast_in_dim.5.mask_ref
  12.5 16.8 %state_exchange.1 = f32[256,128]{1,0:T(8,128)S(1)} custom-call(bf16[256,128]{1,0:T(8,128)(2,1)S(1)} %bitcast.23, f32[256,128]{1,0:T(8,128)S(1)} %reshape_reshape.3.rate_ref, f32[7,128]{1,0:T(8,128)S(1)} %broadcast_in_dim.5.mask_ref), custom_call_target="tpu_custom_call" | custom-call | tf_op jit(solution)/shard_map/state_exchange/pallas_call | solution.py:258
  29.3 0.0 copy-done.1
  29.3 0.0 copy-done.3
  29.3 0.0 copy-done.5
  29.3 0.0 copy-start.4
  29.3 1.6 %copy-done.4 = bf16[512,2048]{1,0:T(8,128)(2,1)S(1)} copy-done((bf16[512,2048]{1,0:T(8,128)(2,1)S(1)}, bf16[512,2048]{1,0:T(8,128)(2,1)}, u32[]{:S(2)}) %copy-start.4) | copy-done | bytes 2097176
  30.9 15.1 %conv.1 = bf16[512,2048]{1,0:T(8,128)(2,1)S(1)} custom-call(f32[512]{0:T(512)S(1)} %convert_subtract_fusion.keep_ref, s32[64]{0:T(128)S(1)} %reduce_max.27.cut_ref, bf16[512,2048]{1,0:T(8,128)(2,1)S(1)} %copy-done.4, bf16[512,2048]{1,0:T(8,128)(2,1)S(1)} %copy-done.1, bf16[512,2048]{1,0:T(8,128)(2,1)S(1)} %copy-done.3, f32[16,16,128]{2,1,0:T(8,128)S(1)} %bitcast.20, ...), custom_call_target="tpu_custom_call" | custom-call | tf_op jit(solution)/shard_map/conv/pallas_call | solution.py:275
  46.0 11.5 %convolution_convert_fusion = bf16[256,4096]{1,0:T(8,128)(2,1)} fusion(bf16[2048,4096]{1,0:T(8,128)(2,1)} %param.15, bf16[512,2048]{1,0:T(8,128)(2,1)S(1)} %conv.1, s32[]{:T(128)S(6)} %select_n.16), kind=kOutput, calls=%fused_computation | convolution fusion | flops 4296015872 | bytes 19922948 | tf_op jit(solution)/shard_map/dot_general | solution.py:293
  57.5 3.3 %collective-permute-start = (bf16[256,4096]{1,0:T(8,128)(2,1)}, bf16[256,4096]{1,0:T(8,128)(2,1)}, u32[]{:S(2)}, u32[]{:S(2)}) collective-permute-start(bf16[256,4096]{1,0:T(8,128)(2,1)} %convolution_convert_fusion), channel_id=1, source_target_pairs={{0,1},{1,0},{2,3},{3,2},{4,5},{5,4},{6,7},{7,6},{8,9},{9,8},{10,11... | collective-permute-start | bytes 6291464 | tf_op jit(solution)/shard_map/ppermute | solution.py:300
  60.8 4.1 %collective-permute-done = bf16[256,4096]{1,0:T(8,128)(2,1)} collective-permute-done((bf16[256,4096]{1,0:T(8,128)(2,1)}, bf16[256,4096]{1,0:T(8,128)(2,1)}, u32[]{:S(2)}, u32[]{:S(2)}) %collective-permute-start) | collective-permute-done | bytes 2097184 | tf_op jit(solution)/shard_map/ppermute | solution.py:300
  64.9 11.8 %add_convert_fusion = bf16[256,4096]{1,0:T(8,128)(2,1)} fusion(bf16[256,4096]{1,0:T(8,128)(2,1)} %collective-permute-done, bf16[2048,4096]{1,0:T(8,128)(2,1)} %param.15, bf16[512,2048]{1,0:T(8,128)(2,1)S(1)} %conv.1, s32[]{:T(128)S(6)} %select_n.15), kind=kOutput, calls=%fused_computation.3 | convolution fusion | flops 4300210176 | bytes 22020100 | tf_op jit(solution)/shard_map/dot_general | solution.py:293
  (3 shorter events, 0.0 us)
Async XLA Ops:
  6.7 1.6 %copy-start = (bf16[512,2048]{1,0:T(8,128)(2,1)S(1)}, bf16[512,2048]{1,0:T(8,128)(2,1)}, u32[]{:S(2)}) copy-start(bf16[512,2048]{1,0:T(8,128)(2,1)} %gate_ref.3) | copy-start | bytes 6291460
  8.3 1.6 %copy-start.2 = (bf16[512,2048]{1,0:T(8,128)(2,1)S(1)}, bf16[512,2048]{1,0:T(8,128)(2,1)}, u32[]{:S(2)}) copy-start(bf16[512,2048]{1,0:T(8,128)(2,1)} %sig_ref.3) | copy-start | bytes 6291460
  9.9 19.4 %copy-start.1 = (bf16[512,2048]{1,0:T(8,128)(2,1)S(1)}, bf16[512,2048]{1,0:T(8,128)(2,1)}, u32[]{:S(2)}) copy-start(bf16[512,2048]{1,0:T(8,128)(2,1)} %gate_ref.3) | copy-start | bytes 6291460
  9.9 19.4 %copy-start.3 = (bf16[512,2048]{1,0:T(8,128)(2,1)S(1)}, bf16[512,2048]{1,0:T(8,128)(2,1)}, u32[]{:S(2)}) copy-start(bf16[512,2048]{1,0:T(8,128)(2,1)} %sig_ref.3) | copy-start | bytes 6291460
  9.9 19.4 %copy-start.5 = (f32[2048]{0:T(1024)S(1)}, f32[2048]{0:T(1024)}, u32[]{:S(2)}) copy-start(f32[2048]{0:T(1024)} %param.14) | copy-start | bytes 24580
  29.3 1.6 %copy-start.4 = (bf16[512,2048]{1,0:T(8,128)(2,1)S(1)}, bf16[512,2048]{1,0:T(8,128)(2,1)}, u32[]{:S(2)}) copy-start(bf16[512,2048]{1,0:T(8,128)(2,1)} %go_ref.1) | copy-start | bytes 6291460
  57.5 7.4 %collective-permute-start = (bf16[256,4096]{1,0:T(8,128)(2,1)}, bf16[256,4096]{1,0:T(8,128)(2,1)}, u32[]{:S(2)}, u32[]{:S(2)}) collective-permute-start(bf16[256,4096]{1,0:T(8,128)(2,1)} %convolution_convert_fusion), channel_id=1, source_target_pairs={{0,1},{1,0},{2,3},{3,2},{4,5},{5,4},{6,7},{7,6},{8,9},{9,8},{10,11... | collective-permute-start | bytes 6291464 | tf_op jit(solution)/shard_map/ppermute | solution.py:300

commit v2 on v1

v2 whole, which is shorter than its diff:
```python
import functools

import jax
import jax.numpy as jnp
from jax import lax
from jax.experimental import pallas as pl
from jax.experimental.pallas import tpu as pltpu
from jax.sharding import PartitionSpec as P

LANES = 128
SUB = 8
STEP = 8
CHUNK = 64
TILE = 512
ROOM = 56 << 20


def fold(dst_ref, src_ref, q, q8, act):
    modes = src_ref.shape[0]
    if q8 > q:
        dst_ref[...] = jnp.zeros_like(dst_ref)
    for j in range(q):
        part = act(src_ref[:, pl.ds(j * LANES, LANES)])
        if modes == 1:
            dst_ref[pl.ds(j, 1), :] = part
        else:
            dst_ref[pl.ds(j, modes, stride=q8), :] = part


def mark(length, docs_ref, keep_ref, cut_ref, last_ref):
    begin = lax.axis_index("ctx") * length

    def clear(i, _):
        for k in range(STEP):
            keep_ref[i * STEP + k] = jnp.float32(1.0)
        cut_ref[i] = jnp.int32(0)
        return 0

    lax.fori_loop(0, length // STEP, clear, 0)
    last_ref[0] = jnp.int32(0)
    at = -begin
    for j in range(docs_ref.shape[0]):

        @pl.when((at >= 0) & (at < length))
        def _():
            keep_ref[at] = jnp.float32(0.0)
            cut_ref[lax.shift_right_logical(at, jnp.int32(STEP.bit_length() - 1))] = jnp.int32(1)
            last_ref[0] = at

        at = at + docs_ref[j]


def recur(modes, q8, h, rows, base, keep_ref, cut_ref, decay_ref, s_ref, x_ref, emit):
    d = [decay_ref[pl.ds(n * q8 + h, SUB), :] for n in range(modes)]

    def run(i, s, cut):
        s = list(s)
        for k in range(STEP):
            at = pl.multiple_of((i * STEP + k) * q8 + h, SUB)
            x = x_ref[pl.ds(at, SUB), :]
            if cut:
                keep = keep_ref[base + i * STEP + k]
                s = [keep * v for v in s]
            for n in range(modes):
                s[n] = d[n] * s[n] + x
            if emit is not None:
                emit(at, x, s)
        return tuple(s)

    def block(i, s):
        return lax.cond(
            cut_ref[base // STEP + i] > 0,
            lambda s: run(i, s, True),
            lambda s: run(i, s, False),
            s,
        )

    out = lax.fori_loop(
        0, rows // STEP, block, tuple(s_ref[pl.ds(n * q8 + h, SUB), :] for n in range(modes))
    )
    for n in range(modes):
        s_ref[pl.ds(n * q8 + h, SUB), :] = out[n]


def end_state_kernel(
    modes, q, q8, length, docs_ref, gate_ref, sig_ref, rates_ref, end_ref, x_ref,
    decay_ref, s_ref, keep_ref, cut_ref, last_ref,
):
    step = pl.program_id(0)
    rows = gate_ref.shape[0]

    @pl.when(step == 0)
    def _():
        s_ref[...] = jnp.zeros_like(s_ref)
        fold(decay_ref, rates_ref, q, q8, lambda a: jnp.exp(-a))
        mark(length, docs_ref, keep_ref, cut_ref, last_ref)

    def tile(i, _):
        t0 = pl.multiple_of(i * 16, 16)
        for j in range(q):
            cols = pl.ds(j * LANES, LANES)
            x = gate_ref[pl.ds(t0, 16), cols].astype(jnp.float32) * sig_ref[
                pl.ds(t0, 16), cols
            ].astype(jnp.float32)
            x_ref[pl.ds(t0 * q8 + j, 16, stride=q8), :] = x
        return 0

    lax.fori_loop(0, rows // 16, tile, 0)

    @pl.when((step + 1) * rows > last_ref[0])
    def _():
        for h in range(0, q8, SUB):
            recur(modes, q8, h, rows, step * rows, keep_ref, cut_ref, decay_ref, s_ref, x_ref, None)

    @pl.when(step == pl.num_programs(0) - 1)
    def _():
        end_ref[...] = s_ref[...].astype(end_ref.dtype)


def exchange_kernel(
    n, length, plan, q, q8, docs_ref, end_ref, rates_ref, out_ref, rate_ref, send_buf, slots,
    send_sem, recv_sem,
):
    me = lax.axis_index("ctx")
    offsets = sorted({off for stage in plan for off, _ in stage})
    barrier = pltpu.get_barrier_semaphore()
    for off in offsets:

        @pl.when(me >= off)
        def _():
            pl.semaphore_signal(
                barrier, inc=1, device_id={"ctx": me - off}, device_id_type=pl.DeviceIdType.MESH
            )

    peers = sum((me + off < n).astype(jnp.int32) for off in offsets)

    @pl.when(me + 1 < n)
    def _():
        pl.semaphore_wait(barrier, peers)

    def copy(k, stage, off):
        src = end_ref if stage == 0 else send_buf.at[stage - 1]
        return pltpu.make_async_remote_copy(
            src_ref=src,
            dst_ref=slots.at[k],
            send_sem=send_sem.at[k],
            recv_sem=recv_sem.at[k],
            device_id={"ctx": jnp.minimum(me + off, n - 1)},
            device_id_type=pl.DeviceIdType.MESH,
        )

    fold(rate_ref, rates_ref, q, q8, lambda a: a)
    start = head = jnp.int32(0)
    for j in range(docs_ref.shape[0]):
        head = jnp.where(start <= me * length, jnp.maximum(head, start), head)
        start = start + docs_ref[j]
    out_ref[...] = jnp.zeros_like(out_ref)
    k0 = 0
    for stage, hops in enumerate(plan):
        if stage:
            send_buf[stage - 1] = out_ref[...].astype(send_buf.dtype)
        for k, (off, gap) in enumerate(hops, k0):

            @pl.when(me + off < n)
            def _():
                copy(k, stage, off).start()

        for k, (off, gap) in enumerate(hops, k0):

            @pl.when(me >= off)
            def _():
                live = jnp.where(head < (me - gap) * length, 1.0, 0.0).astype(jnp.float32)
                weight = jnp.exp(rate_ref[...] * (-float(length * gap))) * live
                copy(k, stage, off).wait_recv()
                out_ref[...] += weight * slots[k].astype(jnp.float32)

        k0 += len(hops)
    k = 0
    for stage, hops in enumerate(plan):
        for off, gap in hops:

            @pl.when(me + off < n)
            def _():
                copy(k, stage, off).wait_send()

            k += 1


def conv_kernel(
    modes, q, q8, length, docs_ref, go_ref, x_ref, rates_ref, res_ref, gain_ref, carried_ref,
    hidden_ref, decay_ref, weight_ref, skip_ref, y_ref, s_ref, keep_ref, cut_ref, last_ref,
):
    step = pl.program_id(0)
    rows = go_ref.shape[0]

    @pl.when(step == 0)
    def _():
        s_ref[...] = carried_ref[...]
        fold(decay_ref, rates_ref, q, q8, lambda a: jnp.exp(-a))
        fold(weight_ref, res_ref, q, q8, lambda a: a)
        fold(skip_ref, gain_ref, q, q8, lambda a: a)
        mark(length, docs_ref, keep_ref, cut_ref, last_ref)

    for h in range(0, q8, SUB):
        r = [weight_ref[pl.ds(n * q8 + h, SUB), :] for n in range(modes)]
        skip = skip_ref[pl.ds(h, SUB), :]

        def emit(at, x, s):
            parts = [skip * x, None, None, None]
            for n in range(modes):
                term = r[n] * s[n]
                p = parts[n % 4]
                parts[n % 4] = term if p is None else p + term
            y_ref[pl.ds(at, SUB), :] = (parts[0] + parts[1]) + (parts[2] + parts[3])

        recur(modes, q8, h, rows, step * rows, keep_ref, cut_ref, decay_ref, s_ref, x_ref, emit)

    def tile(i, _):
        t0 = pl.multiple_of(i * 16, 16)
        for j in range(q):
            cols = pl.ds(j * LANES, LANES)
            y = y_ref[pl.ds(t0 * q8 + j, 16, stride=q8), :]
            g = go_ref[pl.ds(t0, 16), cols].astype(jnp.float32)
            hidden_ref[pl.ds(t0, 16), cols] = (g * y).astype(hidden_ref.dtype)
        return 0

    lax.fori_loop(0, rows // 16, tile, 0)


def project_kernel(hidden_ref, w_ref, out_ref, own_buf, send_buf, recv_buf, send_sem, recv_sem):
    j = pl.program_id(0)
    tiles = own_buf.shape[0]
    half = own_buf.shape[1]
    tile = own_buf.shape[2]
    core = lax.axis_index("tp")

    @pl.when(j == 0)
    def _():
        barrier = pltpu.get_barrier_semaphore()
        pl.semaphore_signal(
            barrier, inc=1, device_id={"tp": 1 - core}, device_id_type=pl.DeviceIdType.MESH
        )
        pl.semaphore_wait(barrier, 1)

    def copy(k):
        return pltpu.make_async_remote_copy(
            src_ref=send_buf.at[k],
            dst_ref=recv_buf.at[k],
            send_sem=send_sem.at[k],
            recv_sem=recv_sem.at[k],
            device_id={"tp": 1 - core},
            device_id_type=pl.DeviceIdType.MESH,
        )

    def product(side):
        rows = pl.ds(pl.multiple_of(side * half, half), half)
        return jnp.dot(
            hidden_ref[rows, :], w_ref[...], preferred_element_type=jnp.float32
        ).astype(jnp.bfloat16)

    def finish(k):
        copy(k).wait_recv()
        out_ref[:, pl.ds(pl.multiple_of(k * tile, tile), tile)] = (
            own_buf[k].astype(jnp.float32) + recv_buf[k].astype(jnp.float32)
        ).astype(out_ref.dtype)

    send_buf[j] = product(1 - core)
    copy(j).start()
    own_buf[j] = product(core)

    @pl.when(j > 0)
    def _():
        finish(j - 1)

    @pl.when(j == tiles - 1)
    def _():
        finish(j)

        def drain(k, _):
            copy(k).wait_send()
            return 0

        lax.fori_loop(0, tiles, drain, 0)


def scan_plan(n):
    plan = [[(off, off - 1) for off in range(1, min(4, n - 1) + 1)]]
    unit = 4
    while unit < n:
        plan.append([(off, off) for off in (unit, 2 * unit, 3 * unit) if off < n])
        unit *= 4
    return plan


def make(n, tp):
    plan = scan_plan(n)
    hops = sum(len(stage) for stage in plan)

    def per_device(gate_out, gate_in, signal, decay_rates, residues, skip_gain, out_proj, doc_lengths):
        length, channels = signal.shape
        modes = decay_rates.shape[0]
        width = out_proj.shape[1]
        q = channels // LANES
        q8 = -(-q // SUB) * SUB
        chunk = min(CHUNK, length)
        flat = (modes * q8, LANES)
        params = pltpu.CompilerParams(vmem_limit_bytes=ROOM)
        smem = pl.BlockSpec(memory_space=pltpu.SMEM)
        vmem = pl.BlockSpec(memory_space=pltpu.VMEM)
        rows = pl.BlockSpec((chunk, channels), lambda i: (i, 0))
        folded = pl.BlockSpec((chunk * q8, LANES), lambda i: (i, 0))
        table = pl.BlockSpec((modes, channels), lambda i: (0, 0))
        state = pl.BlockSpec(flat, lambda i: (0, 0))
        flags = [
            pltpu.SMEM((length,), jnp.float32),
            pltpu.SMEM((length // STEP,), jnp.int32),
            pltpu.SMEM((1,), jnp.int32),
        ]
        end, feed = pl.pallas_call(
            functools.partial(end_state_kernel, modes, q, q8, length),
            grid=(length // chunk,),
            out_shape=[
                jax.ShapeDtypeStruct(flat, jnp.bfloat16),
                jax.ShapeDtypeStruct((length * q8, LANES), jnp.float32),
            ],
            in_specs=[smem, rows, rows, table],
            out_specs=[state, folded],
            scratch_shapes=[pltpu.VMEM(flat, jnp.float32), pltpu.VMEM(flat, jnp.float32)] + flags,
            compiler_params=params,
            name="end_state",
        )(doc_lengths, gate_in, signal, decay_rates)

        carried = pl.pallas_call(
            functools.partial(exchange_kernel, n, length, plan, q, q8),
            out_shape=jax.ShapeDtypeStruct(flat, jnp.float32),
            in_specs=[smem, vmem, vmem],
            out_specs=vmem,
            scratch_shapes=[
                pltpu.VMEM(flat, jnp.float32),
                pltpu.VMEM((max(len(plan) - 1, 1),) + flat, jnp.bfloat16),
                pltpu.VMEM((hops,) + flat, jnp.bfloat16),
                pltpu.SemaphoreType.DMA((hops,)),
                pltpu.SemaphoreType.DMA((hops,)),
            ],
            compiler_params=pltpu.CompilerParams(
                collective_id=0, has_side_effects=True, vmem_limit_bytes=ROOM
            ),
            name="state_exchange",
        )(doc_lengths, end, decay_rates)

        hidden = pl.pallas_call(
            functools.partial(conv_kernel, modes, q, q8, length),
            grid=(length // chunk,),
            out_shape=jax.ShapeDtypeStruct((length, channels), jnp.bfloat16),
            in_specs=[smem, rows, folded, table, table,
                      pl.BlockSpec((1, channels), lambda i: (0, 0)), state],
            out_specs=rows,
            scratch_shapes=[
                pltpu.VMEM(flat, jnp.float32),
                pltpu.VMEM(flat, jnp.float32),
                pltpu.VMEM((q8, LANES), jnp.float32),
                pltpu.VMEM((chunk * q8, LANES), jnp.float32),
                pltpu.VMEM(flat, jnp.float32),
            ] + flags,
            compiler_params=params,
            name="conv",
        )(doc_lengths, gate_out, feed, decay_rates, residues, skip_gain.reshape(1, channels), carried)

        if tp != 2:
            part = jnp.dot(hidden, out_proj, preferred_element_type=jnp.float32)
            return lax.psum_scatter(
                part.astype(jnp.bfloat16), "tp", scatter_dimension=0, tiled=True
            )
        half = length // 2
        tile = min(TILE, width)
        tiles = width // tile
        return pl.pallas_call(
            project_kernel,
            grid=(tiles,),
            out_shape=jax.ShapeDtypeStruct((half, width), jnp.bfloat16),
            in_specs=[
                pl.BlockSpec((length, channels), lambda j: (0, 0)),
                pl.BlockSpec((channels, tile), lambda j: (0, j)),
            ],
            out_specs=pl.BlockSpec((half, width), lambda j: (0, 0)),
            scratch_shapes=[pltpu.VMEM((tiles, half, tile), jnp.bfloat16) for _ in range(3)]
            + [pltpu.SemaphoreType.DMA((tiles,)), pltpu.SemaphoreType.DMA((tiles,))],
            compiler_params=pltpu.CompilerParams(
                collective_id=1, has_side_effects=True, vmem_limit_bytes=ROOM
            ),
            name="project",
        )(hidden, out_proj)

    return per_device


def solution(mesh):
    return jax.shard_map(
        make(mesh.shape["ctx"], mesh.shape["tp"]),
        mesh=mesh,
        in_specs=(
            P("ctx", "tp"),
            P("ctx", "tp"),
            P("ctx", "tp"),
            P(None, "tp"),
            P(None, "tp"),
            P("tp"),
            P("tp", None),
            P(),
        ),
        out_specs=P(("ctx", "tp"), None),
        check_vma=False,
    )
```

time: 76.5 us -> 66.3 us (0.87); the launches traced: 76.7 us -> 65.3 us
  Pallas kernels: 34.4 us -> 62.1 us
  matrix products: 23.3 us -> 0 us
  other arithmetic: 4.69 us -> 0 us
  waiting for transfers between devices: 4.13 us -> 0 us
  local copies, waits for them, and re-layouts: 6.82 us -> 3.13 us
  starting transfers between devices: 3.29 us -> 0 us
    pallas_call x3 -> x4, Pallas kernels: 34.4 us -> 62.1 us  [the longest x1 19.6 us: per_device(): pl.pallas_call(project_kernel, grid=(tiles,), out_shape=jax.ShapeDtypeStr...]
    dot_general x2 -> x0, matrix products: 23.3 us -> none  [project(): jnp.dot(h, out_proj, preferred_element_type=jnp.float32)]
    ppermute x1 -> x0, waiting for transfers between devices: 4.13 us -> none  [per_device(): other = lax.ppermute(other, 'tp', [(0, 1), (1, 0)])]
    ppermute x1 -> x0, starting transfers between devices: 3.29 us -> none  [per_device(): other = lax.ppermute(other, 'tp', [(0, 1), (1, 0)])]
    unnamed x14 -> x1, local copies, waits for them, and re-layouts: 5.74 us -> 3.13 us
    reduce_max x2 -> x0, other arithmetic: 1.49 us -> none  [the longest x1 1.38 us: per_device(): last = jnp.max(jnp.where(inside, local, 0)).astype(jnp.int32).reshape(1)]
    convert_element_type x2 -> x0, other arithmetic: 1.36 us -> none  [the longest x1 1.35 us: per_device(): mask = (head < (me - ids) * length).astype(jnp.float32)]
    unnamed x1 -> x0, other arithmetic: 0.93 us -> none
  transfers between devices with their start and end apart: 1 -> 0, of which waited for: 1 -> 0; matrix products, arithmetic and copies ran while one was open for 0% -> 0% of each run, Pallas kernels for 0% -> 0%
where the time goes in v2:
time: 66.3 us; the launch traced here: 65.3 us
  Pallas kernels  62.1 us (94%)
  local copies, waits for them, and re-layouts  3.13 us (5%)
    pallas_call x1, Pallas kernels, per_device(): pl.pallas_call(project_kernel, grid=(tiles,), out_shape=jax.ShapeDtypeStr...  19.6 us
    pallas_call x1, Pallas kernels, per_device(): pl.pallas_call(functools.partial(conv_kernel, modes, q, q8, length), grid...  17.2 us
    pallas_call x1, Pallas kernels, per_device(): pl.pallas_call(functools.partial(exchange_kernel, n, length, plan, q, q8)...  15.3 us
    pallas_call x1, Pallas kernels, per_device(): pl.pallas_call(functools.partial(end_state_kernel, modes, q, q8, length),...  9.92 us
    unnamed x1, local copies, waits for them, and re-layouts  3.13 us

profile of v2, /device:TPU:31, one launch (start us, length us, event | category | flops | bytes accessed | tf_op | source)
XLA Modules:
  0.0 65.3 jit_solution(16302218174141819515)
XLA Ops:
  0.0 9.9 %end_state.1 = (bf16[256,128]{1,0:T(8,128)(2,1)}, f32[8192,128]{1,0:T(8,128)}) custom-call(s32[8]{0:T(128)} %docs_ref.5, bf16[512,2048]{1,0:T(8,128)(2,1)} %gate_ref.1, bf16[512,2048]{1,0:T(8,128)(2,1)} %sig_ref.1, f32[16,2048]{1,0:T(8,128)} %rates_ref.5), custom_call_target="tpu_custom_call" | custom-call | tf_op jit(solution)/shard_map/end_state/pallas_call | solution.py:319
  9.9 15.3 %state_exchange.1.carried_ref = f32[256,128]{1,0:T(8,128)} custom-call(s32[8]{0:T(128)} %docs_ref.5, bf16[256,128]{1,0:T(8,128)(2,1)} %get-tuple-element.8.end_ref, f32[16,2048]{1,0:T(8,128)} %rates_ref.5), custom_call_target="tpu_custom_call" | custom-call | tf_op jit(solution)/shard_map/state_exchange/pallas_call | solution.py:333
  25.2 17.2 %conv.1.hidden_ref = bf16[512,2048]{1,0:T(8,128)(2,1)} custom-call(s32[8]{0:T(128)} %docs_ref.5, bf16[512,2048]{1,0:T(8,128)(2,1)} %go_ref.1, f32[8192,128]{1,0:T(8,128)} %get-tuple-element.7.x_ref, f32[16,2048]{1,0:T(8,128)} %rates_ref.5, f32[16,2048]{1,0:T(8,128)} %res_ref.1, f32[1,2048]{1,0:T(1,128)} %bitcast.1, f32[256,128]{1,0:T(8,128)} %state_exchange.1.carried_ref), custom_call_target="tpu_custom_call" | custom-call | tf_op jit(solution)/shard_map/conv/pallas_call | solution.py:351
  42.5 19.6 %project.1 = bf16[256,4096]{1,0:T(8,128)(2,1)} custom-call(bf16[512,2048]{1,0:T(8,128)(2,1)} %conv.1.hidden_ref, bf16[2048,4096]{1,0:T(8,128)(2,1)} %w_ref.1), custom_call_target="tpu_custom_call" | custom-call | tf_op jit(solution)/shard_map/project/pallas_call | solution.py:377
  62.1 3.1 %copy.10 = bf16[256,4096]{1,0:T(8,128)(2,1)} copy(bf16[256,4096]{1,0:T(8,128)(2,1)} %project.1) | data formatting | bytes 4194304

commit v3 on v2

--- a/solution.py
+++ b/solution.py
@@ -10,7 +10,8 @@
 LANES = 128
 SUB = 8
 STEP = 8
-CHUNK = 64
+CHUNK = 128
+SPAN = 64
 TILE = 512
 ROOM = 56 << 20
 
@@ -27,64 +28,76 @@
             dst_ref[pl.ds(j, modes, stride=q8), :] = part
 
 
-def mark(length, docs_ref, keep_ref, cut_ref, last_ref):
-    begin = lax.axis_index("ctx") * length
-
+def opens(docs_ref, begin, rows):
+    hit = jnp.int32(0)
+    at = -begin
+    for j in range(docs_ref.shape[0]):
+        hit = jnp.where((at >= 0) & (at < rows), jnp.int32(1), hit)
+        at = at + docs_ref[j]
+    return hit > 0
+
+
+def mark(docs_ref, begin, rows, keep_ref):
     def clear(i, _):
         for k in range(STEP):
             keep_ref[i * STEP + k] = jnp.float32(1.0)
-        cut_ref[i] = jnp.int32(0)
         return 0
 
-    lax.fori_loop(0, length // STEP, clear, 0)
-    last_ref[0] = jnp.int32(0)
+    lax.fori_loop(0, rows // STEP, clear, 0)
     at = -begin
     for j in range(docs_ref.shape[0]):
 
-        @pl.when((at >= 0) & (at < length))
+        @pl.when((at >= 0) & (at < rows))
         def _():
             keep_ref[at] = jnp.float32(0.0)
-            cut_ref[lax.shift_right_logical(at, jnp.int32(STEP.bit_length() - 1))] = jnp.int32(1)
-            last_ref[0] = at
 
         at = at + docs_ref[j]
 
 
-def recur(modes, q8, h, rows, base, keep_ref, cut_ref, decay_ref, s_ref, x_ref, emit):
-    d = [decay_ref[pl.ds(n * q8 + h, SUB), :] for n in range(modes)]
-
-    def run(i, s, cut):
-        s = list(s)
-        for k in range(STEP):
-            at = pl.multiple_of((i * STEP + k) * q8 + h, SUB)
-            x = x_ref[pl.ds(at, SUB), :]
-            if cut:
-                keep = keep_ref[base + i * STEP + k]
-                s = [keep * v for v in s]
+def recur(modes, q8, span, row0, begin, docs_ref, keep_ref, decay_ref, s_ref, x_ref, emitter):
+    def sweep(cut):
+        for h in range(0, q8, SUB):
+            d = [decay_ref[pl.ds(n * q8 + h, SUB), :] for n in range(modes)]
+            emit = emitter(h)
+
+            def run(i, s):
+                s = list(s)
+                for k in range(STEP):
+                    at = pl.multiple_of((row0 + i * STEP + k) * q8 + h, SUB)
+                    x = x_ref[pl.ds(at, SUB), :]
+                    if cut:
+                        keep = keep_ref[i * STEP + k]
+                        s = [keep * v for v in s]
+                    for n in range(modes):
+                        s[n] = d[n] * s[n] + x
+                    if emit is not None:
+                        emit(at, x, s)
+                return tuple(s)
+
+            out = lax.fori_loop(
+                0,
+                span // STEP,
+                run,
+                tuple(s_ref[pl.ds(n * q8 + h, SUB), :] for n in range(modes)),
+            )
             for n in range(modes):
-                s[n] = d[n] * s[n] + x
-            if emit is not None:
-                emit(at, x, s)
-        return tuple(s)
-
-    def block(i, s):
-        return lax.cond(
-            cut_ref[base // STEP + i] > 0,
-            lambda s: run(i, s, True),
-            lambda s: run(i, s, False),
-            s,
-        )
-
-    out = lax.fori_loop(
-        0, rows // STEP, block, tuple(s_ref[pl.ds(n * q8 + h, SUB), :] for n in range(modes))
-    )
-    for n in range(modes):
-        s_ref[pl.ds(n * q8 + h, SUB), :] = out[n]
+                s_ref[pl.ds(n * q8 + h, SUB), :] = out[n]
+
+    hit = opens(docs_ref, begin, span)
+
+    @pl.when(hit)
+    def _():
+        mark(docs_ref, begin, span, keep_ref)
+        sweep(True)
+
+    @pl.when(jnp.logical_not(hit))
+    def _():
+        sweep(False)
 
 
 def end_state_kernel(
-    modes, q, q8, length, docs_ref, gate_ref, sig_ref, rates_ref, end_ref, x_ref,
-    decay_ref, s_ref, keep_ref, cut_ref, last_ref,
+    modes, q, q8, length, docs_ref, gate_ref, sig_ref, rates_ref, end_ref, x_ref, decay_ref,
+    s_ref, keep_ref,
 ):
     step = pl.program_id(0)
     rows = gate_ref.shape[0]
@@ -93,7 +106,6 @@
     def _():
         s_ref[...] = jnp.zeros_like(s_ref)
         fold(decay_ref, rates_ref, q, q8, lambda a: jnp.exp(-a))
-        mark(length, docs_ref, keep_ref, cut_ref, last_ref)
 
     def tile(i, _):
         t0 = pl.multiple_of(i * 16, 16)
@@ -107,10 +119,26 @@
 
     lax.fori_loop(0, rows // 16, tile, 0)
 
-    @pl.when((step + 1) * rows > last_ref[0])
-    def _():
-        for h in range(0, q8, SUB):
-            recur(modes, q8, h, rows, step * rows, keep_ref, cut_ref, decay_ref, s_ref, x_ref, None)
+    begin = lax.axis_index("ctx") * length
+    span = min(SPAN, rows)
+    last = at = -begin
+    for j in range(docs_ref.shape[0]):
+        last = jnp.where(at < length, at, last)
+        at = at + docs_ref[j]
+
+    def piece(p, _):
+        first = step * rows + p * span
+
+        @pl.when(first + span > last)
+        def _():
+            recur(
+                modes, q8, span, p * span, begin + first, docs_ref, keep_ref, decay_ref, s_ref,
+                x_ref, lambda h: None,
+            )
+
+        return 0
+
+    lax.fori_loop(0, rows // span, piece, 0)
 
     @pl.when(step == pl.num_programs(0) - 1)
     def _():
@@ -187,8 +215,8 @@
 
 
 def conv_kernel(
-    modes, q, q8, length, docs_ref, go_ref, x_ref, rates_ref, res_ref, gain_ref, carried_ref,
-    hidden_ref, decay_ref, weight_ref, skip_ref, y_ref, s_ref, keep_ref, cut_ref, last_ref,
+    modes, q, q8, length, docs_ref, go_ref, x_ref, decay_ref, res_ref, gain_ref, carried_ref,
+    hidden_ref, weight_ref, skip_ref, y_ref, s_ref, keep_ref,
 ):
     step = pl.program_id(0)
     rows = go_ref.shape[0]
@@ -196,12 +224,10 @@
     @pl.when(step == 0)
     def _():
         s_ref[...] = carried_ref[...]
-        fold(decay_ref, rates_ref, q, q8, lambda a: jnp.exp(-a))
         fold(weight_ref, res_ref, q, q8, lambda a: a)
         fold(skip_ref, gain_ref, q, q8, lambda a: a)
-        mark(length, docs_ref, keep_ref, cut_ref, last_ref)
-
-    for h in range(0, q8, SUB):
+
+    def emitter(h):
         r = [weight_ref[pl.ds(n * q8 + h, SUB), :] for n in range(modes)]
         skip = skip_ref[pl.ds(h, SUB), :]
 
@@ -213,7 +239,19 @@
                 parts[n % 4] = term if p is None else p + term
             y_ref[pl.ds(at, SUB), :] = (parts[0] + parts[1]) + (parts[2] + parts[3])
 
-        recur(modes, q8, h, rows, step * rows, keep_ref, cut_ref, decay_ref, s_ref, x_ref, emit)
+        return emit
+
+    span = min(SPAN, rows)
+    begin = lax.axis_index("ctx") * length + step * rows
+
+    def piece(p, _):
+        recur(
+            modes, q8, span, p * span, begin + p * span, docs_ref, keep_ref, decay_ref, s_ref,
+            x_ref, emitter,
+        )
+        return 0
+
+    lax.fori_loop(0, rows // span, piece, 0)
 
     def tile(i, _):
         t0 = pl.multiple_of(i * 16, 16)
@@ -227,7 +265,9 @@
     lax.fori_loop(0, rows // 16, tile, 0)
 
 
-def project_kernel(hidden_ref, w_ref, out_ref, own_buf, send_buf, recv_buf, send_sem, recv_sem):
+def project_kernel(
+    hidden_ref, w_ref, out_ref, part_ref, own_buf, send_buf, recv_buf, send_sem, recv_sem
+):
     j = pl.program_id(0)
     tiles = own_buf.shape[0]
     half = own_buf.shape[1]
@@ -252,21 +292,18 @@
             device_id_type=pl.DeviceIdType.MESH,
         )
 
-    def product(side):
-        rows = pl.ds(pl.multiple_of(side * half, half), half)
-        return jnp.dot(
-            hidden_ref[rows, :], w_ref[...], preferred_element_type=jnp.float32
-        ).astype(jnp.bfloat16)
-
     def finish(k):
         copy(k).wait_recv()
         out_ref[:, pl.ds(pl.multiple_of(k * tile, tile), tile)] = (
             own_buf[k].astype(jnp.float32) + recv_buf[k].astype(jnp.float32)
         ).astype(out_ref.dtype)
 
-    send_buf[j] = product(1 - core)
+    part_ref[...] = jnp.dot(
+        hidden_ref[...], w_ref[...], preferred_element_type=jnp.float32
+    ).astype(part_ref.dtype)
+    send_buf[j] = part_ref[pl.ds(pl.multiple_of((1 - core) * half, half), half), :]
     copy(j).start()
-    own_buf[j] = product(core)
+    own_buf[j] = part_ref[pl.ds(pl.multiple_of(core * half, half), half), :]
 
     @pl.when(j > 0)
     def _():
@@ -283,19 +320,16 @@
         lax.fori_loop(0, tiles, drain, 0)
 
 
-def scan_plan(n):
+def scan_plan(n, reach):
     plan = [[(off, off - 1) for off in range(1, min(4, n - 1) + 1)]]
     unit = 4
     while unit < n:
-        plan.append([(off, off) for off in (unit, 2 * unit, 3 * unit) if off < n])
+        plan.append([(off, off) for off in (unit, 2 * unit, 3 * unit) if off < min(n, reach)])
         unit *= 4
     return plan
 
 
 def make(n, tp):
-    plan = scan_plan(n)
-    hops = sum(len(stage) for stage in plan)
-
     def per_device(gate_out, gate_in, signal, decay_rates, residues, skip_gain, out_proj, doc_lengths):
         length, channels = signal.shape
         modes = decay_rates.shape[0]
@@ -311,21 +345,20 @@
         folded = pl.BlockSpec((chunk * q8, LANES), lambda i: (i, 0))
         table = pl.BlockSpec((modes, channels), lambda i: (0, 0))
         state = pl.BlockSpec(flat, lambda i: (0, 0))
-        flags = [
-            pltpu.SMEM((length,), jnp.float32),
-            pltpu.SMEM((length // STEP,), jnp.int32),
-            pltpu.SMEM((1,), jnp.int32),
-        ]
-        end, feed = pl.pallas_call(
+        plan = scan_plan(n, -(-(5 * n * length // 8) // length))
+        hops = sum(len(stage) for stage in plan)
+        flags = [pltpu.SMEM((SPAN,), jnp.float32)]
+        end, feed, decay = pl.pallas_call(
             functools.partial(end_state_kernel, modes, q, q8, length),
             grid=(length // chunk,),
             out_shape=[
                 jax.ShapeDtypeStruct(flat, jnp.bfloat16),
                 jax.ShapeDtypeStruct((length * q8, LANES), jnp.float32),
+                jax.ShapeDtypeStruct(flat, jnp.float32),
             ],
             in_specs=[smem, rows, rows, table],
-            out_specs=[state, folded],
-            scratch_shapes=[pltpu.VMEM(flat, jnp.float32), pltpu.VMEM(flat, jnp.float32)] + flags,
+            out_specs=[state, folded, state],
+            scratch_shapes=[pltpu.VMEM(flat, jnp.float32)] + flags,
             compiler_params=params,
             name="end_state",
         )(doc_lengths, gate_in, signal, decay_rates)
@@ -352,11 +385,10 @@
             functools.partial(conv_kernel, modes, q, q8, length),
             grid=(length // chunk,),
             out_shape=jax.ShapeDtypeStruct((length, channels), jnp.bfloat16),
-            in_specs=[smem, rows, folded, table, table,
+            in_specs=[smem, rows, folded, state, table,
                       pl.BlockSpec((1, channels), lambda i: (0, 0)), state],
             out_specs=rows,
             scratch_shapes=[
-                pltpu.VMEM(flat, jnp.float32),
                 pltpu.VMEM(flat, jnp.float32),
                 pltpu.VMEM((q8, LANES), jnp.float32),
                 pltpu.VMEM((chunk * q8, LANES), jnp.float32),
@@ -364,7 +396,7 @@
             ] + flags,
             compiler_params=params,
             name="conv",
-        )(doc_lengths, gate_out, feed, decay_rates, residues, skip_gain.reshape(1, channels), carried)
+        )(doc_lengths, gate_out, feed, decay, residues, skip_gain.reshape(1, channels), carried)
 
         if tp != 2:
             part = jnp.dot(hidden, out_proj, preferred_element_type=jnp.float32)
@@ -383,7 +415,8 @@
                 pl.BlockSpec((channels, tile), lambda j: (0, j)),
             ],
             out_specs=pl.BlockSpec((half, width), lambda j: (0, 0)),
-            scratch_shapes=[pltpu.VMEM((tiles, half, tile), jnp.bfloat16) for _ in range(3)]
+            scratch_shapes=[pltpu.VMEM((length, tile), jnp.bfloat16)]
+            + [pltpu.VMEM((tiles, half, tile), jnp.bfloat16) for _ in range(3)]
             + [pltpu.SemaphoreType.DMA((tiles,)), pltpu.SemaphoreType.DMA((tiles,))],
             compiler_params=pltpu.CompilerParams(
                 collective_id=1, has_side_effects=True, vmem_limit_bytes=ROOM

time: 66.3 us -> 59.7 us (0.900)
  Pallas kernels: 62.1 us -> 56 us
    pallas_call x1, Pallas kernels: 17.2 us -> 14.2 us  [per_device(): pl.pallas_call(functools.partial(conv_kernel, modes, q, q8, length), grid...]
    pallas_call x1, Pallas kernels: 15.3 us -> 13.6 us  [per_device(): pl.pallas_call(functools.partial(exchange_kernel, n, length, plan, q, q8)...]
    pallas_call x1, Pallas kernels: 9.92 us -> 9.08 us  [per_device(): pl.pallas_call(functools.partial(end_state_kernel, modes, q, q8, length),...]
where the time goes in v3:
time: 59.7 us; the launch traced here: 59.1 us
  Pallas kernels  56 us (94%)
  local copies, waits for them, and re-layouts  3.13 us (5%)
    pallas_call x1, Pallas kernels, per_device(): pl.pallas_call(project_kernel, grid=(tiles,), out_shape=jax.ShapeDtypeStr...  19.1 us
    pallas_call x1, Pallas kernels, per_device(): pl.pallas_call(functools.partial(conv_kernel, modes, q, q8, length), grid...  14.2 us
    pallas_call x1, Pallas kernels, per_device(): pl.pallas_call(functools.partial(exchange_kernel, n, length, plan, q, q8)...  13.6 us
    pallas_call x1, Pallas kernels, per_device(): pl.pallas_call(functools.partial(end_state_kernel, modes, q, q8, length),...  9.08 us
    unnamed x1, local copies, waits for them, and re-layouts  3.13 us

profile of v3, /device:TPU:31, one launch (start us, length us, event | category | flops | bytes accessed | tf_op | source)
XLA Modules:
  0.0 59.1 jit_solution(12836967604780204867)
XLA Ops:
  0.0 9.1 %end_state.1 = (bf16[256,128]{1,0:T(8,128)(2,1)}, f32[8192,128]{1,0:T(8,128)}, f32[256,128]{1,0:T(8,128)}) custom-call(s32[8]{0:T(128)} %docs_ref.5, bf16[512,2048]{1,0:T(8,128)(2,1)} %gate_ref.1, bf16[512,2048]{1,0:T(8,128)(2,1)} %sig_ref.1, f32[16,2048]{1,0:T(8,128)} %rates_ref.3), custom_call_target="tpu_custom_call" | custom-call | tf_op jit(solution)/shard_map/end_state/pallas_call | solution.py:351
  9.1 13.6 %state_exchange.1.carried_ref = f32[256,128]{1,0:T(8,128)} custom-call(s32[8]{0:T(128)} %docs_ref.5, bf16[256,128]{1,0:T(8,128)(2,1)} %get-tuple-element.10.end_ref, f32[16,2048]{1,0:T(8,128)} %rates_ref.3), custom_call_target="tpu_custom_call" | custom-call | tf_op jit(solution)/shard_map/state_exchange/pallas_call | solution.py:366
  22.7 14.2 %conv.1.hidden_ref = bf16[512,2048]{1,0:T(8,128)(2,1)} custom-call(s32[8]{0:T(128)} %docs_ref.5, bf16[512,2048]{1,0:T(8,128)(2,1)} %go_ref.1, f32[8192,128]{1,0:T(8,128)} %get-tuple-element.8.x_ref, f32[256,128]{1,0:T(8,128)} %get-tuple-element.9.decay_ref, f32[16,2048]{1,0:T(8,128)} %res_ref.1, f32[1,2048]{1,0:T(1,128)} %bitcast.1, ...), custom_call_target="tpu_custom_call" | custom-call | tf_op jit(solution)/shard_map/conv/pallas_call | solution.py:384
  36.9 19.1 %project.1 = bf16[256,4096]{1,0:T(8,128)(2,1)} custom-call(bf16[512,2048]{1,0:T(8,128)(2,1)} %conv.1.hidden_ref, bf16[2048,4096]{1,0:T(8,128)(2,1)} %w_ref.1), custom_call_target="tpu_custom_call" | custom-call | tf_op jit(solution)/shard_map/project/pallas_call | solution.py:409
  56.0 3.1 %copy.10 = bf16[256,4096]{1,0:T(8,128)(2,1)} copy(bf16[256,4096]{1,0:T(8,128)(2,1)} %project.1) | data formatting | bytes 4194304

commit v4 on v3

--- a/solution.py
+++ b/solution.py
@@ -14,6 +14,8 @@
 SPAN = 64
 TILE = 512
 ROOM = 56 << 20
+ROOM_CONV = 40 << 20
+ROOM_OUT = 16 << 20
 
 
 def fold(dst_ref, src_ref, q, q8, act):
@@ -216,10 +218,12 @@
 
 def conv_kernel(
     modes, q, q8, length, docs_ref, go_ref, x_ref, decay_ref, res_ref, gain_ref, carried_ref,
-    hidden_ref, weight_ref, skip_ref, y_ref, s_ref, keep_ref,
+    w_ref, hidden_ref, near_ref, weight_ref, skip_ref, y_ref, s_ref, keep_ref, w_sem,
 ):
     step = pl.program_id(0)
     rows = go_ref.shape[0]
+    fetch = pltpu.make_async_copy(w_ref, near_ref, w_sem)
+    pl.when(step == 0)(fetch.start)
 
     @pl.when(step == 0)
     def _():
@@ -263,24 +267,21 @@
         return 0
 
     lax.fori_loop(0, rows // 16, tile, 0)
+    pl.when(step == pl.num_programs(0) - 1)(fetch.wait)
 
 
 def project_kernel(
     hidden_ref, w_ref, out_ref, part_ref, own_buf, send_buf, recv_buf, send_sem, recv_sem
 ):
-    j = pl.program_id(0)
     tiles = own_buf.shape[0]
     half = own_buf.shape[1]
     tile = own_buf.shape[2]
     core = lax.axis_index("tp")
-
-    @pl.when(j == 0)
-    def _():
-        barrier = pltpu.get_barrier_semaphore()
-        pl.semaphore_signal(
-            barrier, inc=1, device_id={"tp": 1 - core}, device_id_type=pl.DeviceIdType.MESH
-        )
-        pl.semaphore_wait(barrier, 1)
+    barrier = pltpu.get_barrier_semaphore()
+    pl.semaphore_signal(
+        barrier, inc=1, device_id={"tp": 1 - core}, device_id_type=pl.DeviceIdType.MESH
+    )
+    pl.semaphore_wait(barrier, 1)
 
     def copy(k):
         return pltpu.make_async_remote_copy(
@@ -298,26 +299,29 @@
             own_buf[k].astype(jnp.float32) + recv_buf[k].astype(jnp.float32)
         ).astype(out_ref.dtype)
 
-    part_ref[...] = jnp.dot(
-        hidden_ref[...], w_ref[...], preferred_element_type=jnp.float32
-    ).astype(part_ref.dtype)
-    send_buf[j] = part_ref[pl.ds(pl.multiple_of((1 - core) * half, half), half), :]
-    copy(j).start()
-    own_buf[j] = part_ref[pl.ds(pl.multiple_of(core * half, half), half), :]
-
-    @pl.when(j > 0)
-    def _():
-        finish(j - 1)
-
-    @pl.when(j == tiles - 1)
-    def _():
-        finish(j)
-
-        def drain(k, _):
-            copy(k).wait_send()
-            return 0
-
-        lax.fori_loop(0, tiles, drain, 0)
+    def step(j, _):
+        cols = pl.ds(pl.multiple_of(j * tile, tile), tile)
+        part_ref[...] = jnp.dot(
+            hidden_ref[...], w_ref[:, cols], preferred_element_type=jnp.float32
+        ).astype(part_ref.dtype)
+        send_buf[j] = part_ref[pl.ds(pl.multiple_of((1 - core) * half, half), half), :]
+        copy(j).start()
+        own_buf[j] = part_ref[pl.ds(pl.multiple_of(core * half, half), half), :]
+
+        @pl.when(j > 0)
+        def _():
+            finish(j - 1)
+
+        return 0
+
+    lax.fori_loop(0, tiles, step, 0)
+    finish(tiles - 1)
+
+    def drain(k, _):
+        copy(k).wait_send()
+        return 0
+
+    lax.fori_loop(0, tiles, drain, 0)
 
 
 def scan_plan(n, reach):
@@ -381,25 +385,30 @@
             name="state_exchange",
         )(doc_lengths, end, decay_rates)
 
-        hidden = pl.pallas_call(
+        hidden, near = pl.pallas_call(
             functools.partial(conv_kernel, modes, q, q8, length),
             grid=(length // chunk,),
-            out_shape=jax.ShapeDtypeStruct((length, channels), jnp.bfloat16),
+            out_shape=[
+                pltpu.VMEM((length, channels), jnp.bfloat16),
+                pltpu.VMEM(out_proj.shape, out_proj.dtype),
+            ],
             in_specs=[smem, rows, folded, state, table,
-                      pl.BlockSpec((1, channels), lambda i: (0, 0)), state],
-            out_specs=rows,
+                      pl.BlockSpec((1, channels), lambda i: (0, 0)), state,
+                      pl.BlockSpec(memory_space=pltpu.HBM)],
+            out_specs=[rows, pl.BlockSpec(memory_space=pl.ANY)],
             scratch_shapes=[
                 pltpu.VMEM(flat, jnp.float32),
                 pltpu.VMEM((q8, LANES), jnp.float32),
                 pltpu.VMEM((chunk * q8, LANES), jnp.float32),
                 pltpu.VMEM(flat, jnp.float32),
-            ] + flags,
-            compiler_params=params,
+            ] + flags + [pltpu.SemaphoreType.DMA],
+            compiler_params=pltpu.CompilerParams(vmem_limit_bytes=ROOM_CONV),
             name="conv",
-        )(doc_lengths, gate_out, feed, decay, residues, skip_gain.reshape(1, channels), carried)
+        )(doc_lengths, gate_out, feed, decay, residues, skip_gain.reshape(1, channels), carried,
+          out_proj)
 
         if tp != 2:
-            part = jnp.dot(hidden, out_proj, preferred_element_type=jnp.float32)
+            part = jnp.dot(hidden, near, preferred_element_type=jnp.float32)
             return lax.psum_scatter(
                 part.astype(jnp.bfloat16), "tp", scatter_dimension=0, tiled=True
             )
@@ -408,21 +417,17 @@
         tiles = width // tile
         return pl.pallas_call(
             project_kernel,
-            grid=(tiles,),
             out_shape=jax.ShapeDtypeStruct((half, width), jnp.bfloat16),
-            in_specs=[
-                pl.BlockSpec((length, channels), lambda j: (0, 0)),
-                pl.BlockSpec((channels, tile), lambda j: (0, j)),
-            ],
-            out_specs=pl.BlockSpec((half, width), lambda j: (0, 0)),
+            in_specs=[vmem, vmem],
+            out_specs=vmem,
             scratch_shapes=[pltpu.VMEM((length, tile), jnp.bfloat16)]
             + [pltpu.VMEM((tiles, half, tile), jnp.bfloat16) for _ in range(3)]
             + [pltpu.SemaphoreType.DMA((tiles,)), pltpu.SemaphoreType.DMA((tiles,))],
             compiler_params=pltpu.CompilerParams(
-                collective_id=1, has_side_effects=True, vmem_limit_bytes=ROOM
+                collective_id=1, has_side_effects=True, vmem_limit_bytes=ROOM_OUT
             ),
             name="project",
-        )(hidden, out_proj)
+        )(hidden, near)
 
     return per_device
 

time: 59.7 us -> 53.4 us (0.89)
  Pallas kernels: 56 us -> 51.9 us
  local copies, waits for them, and re-layouts: 3.13 us -> 1.32 us
    pallas_call x1, Pallas kernels: 19.1 us -> 15.6 us  [per_device(): pl.pallas_call(project_kernel, out_shape=jax.ShapeDtypeStruct((half, widt...]
    pallas_call x1, Pallas kernels: 9.08 us -> 6.7 us  [per_device(): pl.pallas_call(functools.partial(end_state_kernel, modes, q, q8, length),...]
    unnamed x1, local copies, waits for them, and re-layouts: 3.13 us -> 1.32 us
    pallas_call x1, Pallas kernels: 13.6 us -> 15.3 us  [per_device(): pl.pallas_call(functools.partial(exchange_kernel, n, length, plan, q, q8)...]
where the time goes in v4:
time: 53.4 us; the launch traced here: 53.2 us
  Pallas kernels  51.9 us (97%)
  local copies, waits for them, and re-layouts  1.32 us (2%)
    pallas_call x1, Pallas kernels, per_device(): pl.pallas_call(project_kernel, out_shape=jax.ShapeDtypeStruct((half, widt...  15.6 us
    pallas_call x1, Pallas kernels, per_device(): pl.pallas_call(functools.partial(exchange_kernel, n, length, plan, q, q8)...  15.3 us
    pallas_call x1, Pallas kernels, per_device(): pl.pallas_call(functools.partial(conv_kernel, modes, q, q8, length), grid...  14.2 us
    pallas_call x1, Pallas kernels, per_device(): pl.pallas_call(functools.partial(end_state_kernel, modes, q, q8, length),...  6.7 us
    unnamed x1, local copies, waits for them, and re-layouts  1.32 us

profile of v4, /device:TPU:31, one launch (start us, length us, event | category | flops | bytes accessed | tf_op | source)
XLA Modules:
  0.0 53.2 jit_solution(15615561092182836755)
XLA Ops:
  0.0 6.7 %end_state.1 = (bf16[256,128]{1,0:T(8,128)(2,1)}, f32[8192,128]{1,0:T(8,128)}, f32[256,128]{1,0:T(8,128)}) custom-call(s32[8]{0:T(128)} %docs_ref.5, bf16[512,2048]{1,0:T(8,128)(2,1)} %gate_ref.1, bf16[512,2048]{1,0:T(8,128)(2,1)} %sig_ref.1, f32[16,2048]{1,0:T(8,128)} %rates_ref.3), custom_call_target="tpu_custom_call" | custom-call | tf_op jit(solution)/shard_map/end_state/pallas_call | solution.py:355
  6.7 15.3 %state_exchange.1.carried_ref = f32[256,128]{1,0:T(8,128)} custom-call(s32[8]{0:T(128)} %docs_ref.5, bf16[256,128]{1,0:T(8,128)(2,1)} %get-tuple-element.12.end_ref, f32[16,2048]{1,0:T(8,128)} %rates_ref.3), custom_call_target="tpu_custom_call" | custom-call | tf_op jit(solution)/shard_map/state_exchange/pallas_call | solution.py:370
  22.0 14.2 %conv.1 = (bf16[512,2048]{1,0:T(8,128)(2,1)S(1)}, bf16[2048,4096]{1,0:T(8,128)(2,1)S(1)}) custom-call(s32[8]{0:T(128)} %docs_ref.5, bf16[512,2048]{1,0:T(8,128)(2,1)} %go_ref.1, f32[8192,128]{1,0:T(8,128)} %get-tuple-element.10.x_ref, f32[256,128]{1,0:T(8,128)} %get-tuple-element.11.decay_ref, f32[16,2048]{1,0:T(8,128)} %res_ref.1, f32[1,2048]{1,0:T(1,128)} %bitcast.1, ...), custom_call_target="tpu_custom_call" | custom-call | tf_op jit(solution)/shard_map/conv/pallas_call | solution.py:388
  36.3 15.6 %project.1 = bf16[256,4096]{1,0:T(8,128)(2,1)S(1)} custom-call(bf16[512,2048]{1,0:T(8,128)(2,1)S(1)} %get-tuple-element.13.hidden_ref, bf16[2048,4096]{1,0:T(8,128)(2,1)S(1)} %get-tuple-element.14.w_ref), custom_call_target="tpu_custom_call" | custom-call | tf_op jit(solution)/shard_map/project/pallas_call | solution.py:418
  51.9 1.3 %copy.10 = bf16[256,4096]{1,0:T(8,128)(2,1)} copy(bf16[256,4096]{1,0:T(8,128)(2,1)S(1)} %project.1) | data formatting | bytes 4194304

commit v5 on v4

--- a/solution.py
+++ b/solution.py
@@ -9,7 +9,7 @@
 
 LANES = 128
 SUB = 8
-STEP = 8
+STEP = 16
 CHUNK = 128
 SPAN = 64
 TILE = 512

time: 53.4 us -> 52.4 us (0.981)
  Pallas kernels: 51.9 us -> 50.4 us
    pallas_call x1, Pallas kernels: 15.3 us -> 12.9 us  [per_device(): pl.pallas_call(functools.partial(exchange_kernel, n, length, plan, q, q8)...]
    pallas_call x1, Pallas kernels: 6.7 us -> 7.81 us  [per_device(): pl.pallas_call(functools.partial(end_state_kernel, modes, q, q8, length),...]
where the time goes in v5:
time: 52.4 us; the launch traced here: 51.7 us
  Pallas kernels  50.4 us (96%)
  local copies, waits for them, and re-layouts  1.32 us (3%)
    pallas_call x1, Pallas kernels, per_device(): pl.pallas_call(project_kernel, out_shape=jax.ShapeDtypeStruct((half, widt...  15.7 us
    pallas_call x1, Pallas kernels, per_device(): pl.pallas_call(functools.partial(conv_kernel, modes, q, q8, length), grid...  13.9 us
    pallas_call x1, Pallas kernels, per_device(): pl.pallas_call(functools.partial(exchange_kernel, n, length, plan, q, q8)...  12.9 us
    pallas_call x1, Pallas kernels, per_device(): pl.pallas_call(functools.partial(end_state_kernel, modes, q, q8, length),...  7.81 us
    unnamed x1, local copies, waits for them, and re-layouts  1.32 us

profile of v5, /device:TPU:31, one launch (start us, length us, event | category | flops | bytes accessed | tf_op | source)
XLA Modules:
  0.0 51.7 jit_solution(6850409557247907732)
XLA Ops:
  0.0 7.8 %end_state.1 = (bf16[256,128]{1,0:T(8,128)(2,1)}, f32[8192,128]{1,0:T(8,128)}, f32[256,128]{1,0:T(8,128)}) custom-call(s32[8]{0:T(128)} %docs_ref.5, bf16[512,2048]{1,0:T(8,128)(2,1)} %gate_ref.1, bf16[512,2048]{1,0:T(8,128)(2,1)} %sig_ref.1, f32[16,2048]{1,0:T(8,128)} %rates_ref.3), custom_call_target="tpu_custom_call" | custom-call | tf_op jit(solution)/shard_map/end_state/pallas_call | solution.py:355
  7.8 12.9 %state_exchange.1.carried_ref = f32[256,128]{1,0:T(8,128)} custom-call(s32[8]{0:T(128)} %docs_ref.5, bf16[256,128]{1,0:T(8,128)(2,1)} %get-tuple-element.12.end_ref, f32[16,2048]{1,0:T(8,128)} %rates_ref.3), custom_call_target="tpu_custom_call" | custom-call | tf_op jit(solution)/shard_map/state_exchange/pallas_call | solution.py:370
  20.7 13.9 %conv.1 = (bf16[512,2048]{1,0:T(8,128)(2,1)S(1)}, bf16[2048,4096]{1,0:T(8,128)(2,1)S(1)}) custom-call(s32[8]{0:T(128)} %docs_ref.5, bf16[512,2048]{1,0:T(8,128)(2,1)} %go_ref.1, f32[8192,128]{1,0:T(8,128)} %get-tuple-element.10.x_ref, f32[256,128]{1,0:T(8,128)} %get-tuple-element.11.decay_ref, f32[16,2048]{1,0:T(8,128)} %res_ref.1, f32[1,2048]{1,0:T(1,128)} %bitcast.1, ...), custom_call_target="tpu_custom_call" | custom-call | tf_op jit(solution)/shard_map/conv/pallas_call | solution.py:388
  34.7 15.7 %project.1 = bf16[256,4096]{1,0:T(8,128)(2,1)S(1)} custom-call(bf16[512,2048]{1,0:T(8,128)(2,1)S(1)} %get-tuple-element.13.hidden_ref, bf16[2048,4096]{1,0:T(8,128)(2,1)S(1)} %get-tuple-element.14.w_ref), custom_call_target="tpu_custom_call" | custom-call | tf_op jit(solution)/shard_map/project/pallas_call | solution.py:418
  50.4 1.3 %copy.10 = bf16[256,4096]{1,0:T(8,128)(2,1)} copy(bf16[256,4096]{1,0:T(8,128)(2,1)S(1)} %project.1) | data formatting | bytes 4194304
